TPU v7x, 32 devices: a whole 2x2x4 slice. The times are simulated.
32 devices in a mesh: ctx: 16 (over z, y, x), head: 2 (over core).
Axes of the slice: x: 2, y: 2, z: 4, core: 2. Of those that a mesh axis runs over, the one named last changes fastest.
Arguments:
- lin_query: bfloat16 [2048, 64, 128], P('ctx', 'head'), may hold values from -6 to 6
- lin_key: bfloat16 [2048, 64, 128], P('ctx', 'head'), may hold values from -6 to 6
- lin_value: bfloat16 [2048, 64, 128], P('ctx', 'head'), may hold values from -18 to 18
- log_decay: float32 [64, 2048], P('head', 'ctx'), may hold values from -1 to 0
- norm_gain: float32 [64, 128], P('head'), may hold values from 0.5 to 1.5
- attn_query: bfloat16 [2048, 64, 128], P('ctx', 'head'), may hold values from -30 to 30
- attn_key: bfloat16 [2048, 8, 128], P('ctx', 'head'), may hold values from -16 to 16
- attn_value: bfloat16 [2048, 8, 128], P('ctx', 'head'), may hold values from -6 to 6
Outputs:
- lin_out: bfloat16 [2048, 64, 128], P('ctx', 'head')
- attn_out: bfloat16 [2048, 64, 128], P('ctx', 'head')
All inputs are finite; a program needn't handle non-finite values.
Results may differ from a plain program's by a relative error of at most 0.0055.
Values may be sent and summed in bfloat16 or wider, within the bound.
A program may use at most 192 MiB of HBM per device.

v0:
```python
import jax
import jax.numpy as jnp
from jax import lax
from jax.sharding import PartitionSpec as P

QUERY_HEADS = 64
HD = 128


def carried_in(x, axis, combine, identity):
    size, mine = (lax.axis_size(axis), lax.axis_index(axis))
    everything = jax.tree.map(lambda part: lax.all_gather(part, axis), x)
    start = jax.tree.map(
        lambda part, zero: jnp.broadcast_to(jnp.asarray(zero, part.dtype), part.shape), x, identity
    )

    def hop(k, before):
        reached = k < mine
        new = combine(before, jax.tree.map(lambda part: part[k], everything))
        return jax.tree.map(lambda a, b: jnp.where(reached, a, b), new, before)

    return lax.fori_loop(0, size, hop, start)


def act_round(values):
    return jax.nn.silu(values.astype(jnp.float32)).astype(jnp.bfloat16)


def chain_state(earlier, later):
    decay_early, state_early = earlier
    decay_late, state_late = later
    return (decay_early * decay_late, decay_late[:, None, None] * state_early + state_late)


def lightning(lin_query, lin_key, lin_value, log_decay, norm_gain):
    act_query = act_round(lin_query)
    act_key = act_round(lin_key)
    act_value = act_round(lin_value)
    token_position = jnp.arange(lin_query.shape[0])
    cumulative = jnp.cumsum(log_decay, axis=1)
    causal = token_position[:, None] >= token_position[None, :]
    spread = cumulative[:, :, None] - cumulative[:, None, :]
    decay_matrix = jnp.exp(jnp.where(causal[None], spread, -1e30))
    scores = jnp.einsum("thd,shd->hts", act_query, act_key, preferred_element_type=jnp.float32)
    weights = (scores * decay_matrix).astype(jnp.bfloat16)
    inner_part = jnp.einsum("hts,shd->thd", weights, act_value, preferred_element_type=jnp.float32)
    last_sum = cumulative[:, -1]
    key_factor = jnp.exp(last_sum[None, :] - cumulative.T)
    scaled_keys = (act_key.astype(jnp.float32) * key_factor[:, :, None]).astype(jnp.bfloat16)
    local_state = jnp.einsum(
        "shd,she->hde", scaled_keys, act_value, preferred_element_type=jnp.float32
    )
    identity = (jnp.ones_like(last_sum), jnp.zeros_like(local_state))
    prior_decay, prior_state = carried_in(
        (jnp.exp(last_sum), local_state), "ctx", chain_state, identity
    )
    outer_part = jnp.einsum(
        "thd,hde->the", act_query.astype(jnp.float32), prior_state, precision=lax.Precision.HIGHEST
    )
    mixed_out = inner_part + outer_part * jnp.exp(cumulative.T)[:, :, None]
    row_squares = jnp.sum(mixed_out * mixed_out, axis=(1, 2))
    total_squares = lax.psum(row_squares, "head")
    inverse = lax.rsqrt(total_squares / (QUERY_HEADS * HD) + 1e-06)
    return (mixed_out * inverse[:, None, None] * norm_gain[None]).astype(jnp.bfloat16)


def to_groups(query_rows, kv_local):
    rows = query_rows.shape[0]
    group = query_rows.shape[1] // kv_local
    shaped = query_rows.reshape(rows, kv_local, group, query_rows.shape[2]).transpose(1, 0, 2, 3)
    return shaped.reshape(kv_local, rows * group, query_rows.shape[2])


def from_groups(grouped, rows):
    kv_local = grouped.shape[0]
    group = grouped.shape[1] // rows
    shaped = grouped.reshape(kv_local, rows, group, grouped.shape[2]).transpose(1, 0, 2, 3)
    return shaped.reshape(rows, kv_local * group, grouped.shape[2])


def attend(state_now, group_query, positions, key_piece, value_piece):
    running_max, totals, accumulated = state_now
    scores = jnp.einsum(
        "gqd,pgd->gqp", group_query, key_piece, preferred_element_type=jnp.float32
    ) * HD ** (-0.5)
    key_pos = jnp.arange(key_piece.shape[0])
    visible = positions[:, None] >= key_pos[None, :]
    masked = jnp.where(visible[None], scores, -1e30)
    newest = jnp.maximum(running_max, jnp.max(masked, axis=2))
    prob_rows = jnp.where(visible[None], jnp.exp(scores - newest[:, :, None]), 0.0)
    totals = jnp.sum(prob_rows, axis=2)
    accumulated = jnp.einsum(
        "gqp,pgd->gqd",
        prob_rows.astype(jnp.bfloat16),
        value_piece,
        preferred_element_type=jnp.float32,
    )
    return (newest, totals, accumulated)


def softmax_part(attn_query, attn_key, attn_value):
    length = attn_query.shape[0]
    kv_local = attn_key.shape[1]
    group = attn_query.shape[1] // kv_local
    ctx_index = lax.axis_index("ctx")
    own_pos = ctx_index * length + jnp.arange(length)
    query_sets = [(to_groups(attn_query, kv_local), jnp.repeat(own_pos, group), length)]

    def empty_state(group_query):
        shape_rows = group_query.shape[:2]
        return (
            jnp.full(shape_rows, -1e30, jnp.float32),
            jnp.zeros(shape_rows, jnp.float32),
            jnp.zeros(group_query.shape, jnp.float32),
        )

    initial = tuple((empty_state(query_set[0]) for query_set in query_sets))
    key_piece = lax.all_gather(attn_key, "ctx", axis=0, tiled=True)
    value_piece = lax.all_gather(attn_value, "ctx", axis=0, tiled=True)
    results = []
    for query_set, state_now in zip(query_sets, initial):
        group_query, positions, set_rows = query_set
        state_now = attend(state_now, group_query, positions, key_piece, value_piece)
        results.append(state_now)
    finals = tuple(results)
    running_max, totals, accumulated = finals[0]
    grouped = (accumulated / totals[:, :, None]).astype(jnp.bfloat16)
    result = from_groups(grouped, length)
    return result


def local(lin_query, lin_key, lin_value, log_decay, norm_gain, attn_query, attn_key, attn_value):
    lin_out = lightning(lin_query, lin_key, lin_value, log_decay, norm_gain)
    attn_out = softmax_part(attn_query, attn_key, attn_value)
    return (lin_out, attn_out)


def solution(mesh):
    return jax.shard_map(
        local,
        mesh=mesh,
        in_specs=(
            P("ctx", "head", None),
            P("ctx", "head", None),
            P("ctx", "head", None),
            P("head", "ctx"),
            P("head", None),
            P("ctx", "head", None),
            P("ctx", "head", None),
            P("ctx", "head", None),
        ),
        out_specs=(P("ctx", "head", None), P("ctx", "head", None)),
        check_vma=False,
    )
```

profile of v0, /device:TPU:29, one launch (start us, length us, event | category | flops | bytes accessed | tf_op | source)
XLA Modules:
  0.0 538.0 jit_solution(17217921467654826165)
XLA Ops:
  12.1 2.6 multiply_convert_fusion.1
  17.7 2.2 fusion.23
  21.9 29.0 %all-reduce = f32[512]{0:T(512)S(1)} all-reduce(f32[512]{0:T(512)S(1)} %dynamic-update-slice), channel_id=2, replica_groups=mesh['ctx'=16,'head'=2] {'ctx'}, use_global_device_ids=true, to_apply=%add | all-reduce | flops 512 | bytes 4096
  51.2 5.2 fusion.19
  56.5 2.7 iota_compare_fusion
  59.1 11.9 %all-gather.6.cloned.1.call-done = bf16[2048,4,128]{2,0,1:T(8,128)(2,1)} async-done(((bf16[128,4,128]{2,0,1:T(8,128)(2,1)}), bf16[2048,4,128]{2,0,1:T(8,128)(2,1)}) %all-gather.6.cloned.1.call-update) | async-done | bytes 2097168 | tf_op jit(solution)/shard_map/all_gather | solution.py:118
  71.0 16.4 %select_reduce_fusion = (f32[4,1024]{1,0:T(4,128)S(1)}, f32[4,1024,2048]{2,1,0:T(8,128)}) fusion(pred[1024,2048]{1,0:T(8,128)(4,1)} %iota_compare_fusion, bf16[2048,4,128]{2,0,1:T(8,128)(2,1)} %all-gather.6.cloned.1.call-done, bf16[128,32,128]{2,1,0:T(8,128)(2,1)S(1)} %copy-done), kind=kOutput, calls=%fused_computation.4 | convolution fusion | flops 2172645376 | bytes 38813696 | tf_op jit(solution)/shard_map/gqd,pgd->gqp/dot_general | solution.py:83
  87.4 15.3 %fusion.1 = f32[4,1024]{1,0:T(4,128)S(1)} fusion(f32[4,1024,2048]{2,1,0:T(8,128)} %get-tuple-element.140, f32[4,1024]{1,0:T(4,128)S(1)} %broadcast_maximum_fusion, pred[1024,2048]{1,0:T(8,128)(4,1)S(1)} %copy-done.2), kind=kLoop, calls=%fused_computation.5 | loop fusion | flops 33550336 | bytes 35684352 | tf_op jit(solution)/shard_map/reduce_sum | solution.py:91
  102.7 30.7 %all-gather.8.cloned.1.call-done = bf16[2048,4,128]{2,0,1:T(8,128)(2,1)} async-done(((bf16[128,4,128]{2,0,1:T(8,128)(2,1)}), bf16[2048,4,128]{2,0,1:T(8,128)(2,1)}) %all-gather.8.cloned.1.call-update) | async-done | bytes 2097168 | tf_op jit(solution)/shard_map/all_gather | solution.py:119
  133.4 15.1 %fusion.30 = bf16[128,4,8,128]{3,2,0,1:T(8,128)(2,1)S(1)} fusion(f32[4,1024]{1,0:T(4,128)S(1)} %fusion.1, bf16[2048,4,128]{2,0,1:T(8,128)(2,1)} %all-gather.8.cloned.1.call-done, f32[4,1024,2048]{2,1,0:T(8,128)} %get-tuple-element.140, f32[4,1024]{1,0:T(4,128)S(1)} %broadcast_maximum_fusion, pred[1024,2048]{1,0:T(8,128)(4,1)} %iota_compare_fusion), kind=kOutput, calls=%fused_computation.46 | convolution fusion | flops 2182086656 | bytes 38830080 | tf_op jit(solution)/shard_map/gqp,pgd->gqd/dot_general | solution.py:92
  149.6 336.3 %all-gather.10.cloned.1.call-done = f32[512,128,128]{2,1,0:T(8,128)} async-done(((f32[32,128,128]{2,1,0:T(8,128)}), f32[512,128,128]{2,1,0:T(8,128)}) %all-gather.10.cloned.1.call-update) | async-done | bytes 33554448 | tf_op jit(solution)/shard_map/all_gather | solution.py:12
  485.9 34.4 %while.14 = (s32[]{:T(128)}, f32[32,128,128]{2,1,0:T(8,128)S(1)}, s32[]{:T(128)}, f32[16,32]{1,0:T(8,128)S(1)}, f32[16,32,128,128]{3,2,1,0:T(8,128)}, /*index=5*/s32[]{:T(128)}, s32[]{:T(128)}) while((s32[]{:T(128)}, f32[32,128,128]{2,1,0:T(8,128)S(1)}, s32[]{:T(128)}, f32[16,32]{1,0:T(8,128)S(1)}, f32[16,32,128,128]{3,2,1,0:T(8,128)}, ...), condition=%wide.region_2.3_spmd.clone, body=%wide.region_1.2_spmd.clone.sunk | while | flops 2097156 | bytes 6291945 | solution.py:22
  485.9 2.2 fusion.48
  488.2 2.1 fusion.48
  490.3 2.1 fusion.48
  492.4 2.1 fusion.48
  494.6 2.1 fusion.48
  496.7 2.1 fusion.48
  498.8 2.1 fusion.48
  501.0 2.1 fusion.48
  503.1 2.1 fusion.48
  515.9 2.1 fusion.48
  520.4 4.8 multiply_reduce_fusion
  525.2 2.6 psum.7
  (67 shorter events, 27.2 us)
Async XLA Ops:
  7.2 63.8 %copy-start = (bf16[128,32,128]{2,1,0:T(8,128)(2,1)S(1)}, bf16[128,32,128]{2,1,0:T(8,128)(2,1)}, u32[]{:S(2)}) copy-start(bf16[128,32,128]{2,1,0:T(8,128)(2,1)} %param.15) | copy-start | bytes 3145732
  7.2 7.5 %copy-start.6 = (bf16[128,32,128]{2,1,0:T(8,128)(2,1)S(1)}, bf16[128,32,128]{2,1,0:T(8,128)(2,1)}, u32[]{:S(2)}) copy-start(bf16[128,32,128]{2,1,0:T(8,128)(2,1)} %param.10) | copy-start | bytes 3145732
  7.2 7.5 %copy-start.5 = (bf16[128,32,128]{2,1,0:T(8,128)(2,1)S(1)}, bf16[128,32,128]{2,1,0:T(8,128)(2,1)}, u32[]{:S(2)}) copy-start(bf16[128,32,128]{2,1,0:T(8,128)(2,1)} %param.12) | copy-start | bytes 3145732
  7.2 63.8 %all-gather.6.cloned.1.call-start = ((), (), s32[]{:S(2)}) async-start(), calls=%async_computation | async-start | bytes 2228224 | tf_op jit(solution)/shard_map/all_gather | solution.py:118
  9.0 124.4 %all-gather.8.cloned.1.call-start = ((), (), s32[]{:S(2)}) async-start(), calls=%async_computation.1 | async-start | bytes 2228224 | tf_op jit(solution)/shard_map/all_gather | solution.py:119
  10.6 475.3 %all-gather.10.cloned.1.call-start = ((), (), s32[]{:S(2)}) async-start(), calls=%async_computation.2 | async-start | bytes 35651584 | tf_op jit(solution)/shard_map/all_gather | solution.py:12
  16.7 1.0 copy-start.3
  19.9 0.7 copy-start.8
  71.0 16.4 %copy-start.2 = (pred[1024,2048]{1,0:T(8,128)(4,1)S(1)}, pred[1024,2048]{1,0:T(8,128)(4,1)}, u32[]{:S(2)}) copy-start(pred[1024,2048]{1,0:T(8,128)(4,1)} %iota_compare_fusion) | copy-start | bytes 6291460
  485.9 34.4 %copy-start.4 = (bf16[128,32,128]{2,1,0:T(8,128)(2,1)S(1)}, bf16[128,32,128]{2,1,0:T(8,128)(2,1)}, u32[]{:S(2)}) copy-start(bf16[128,32,128]{2,1,0:T(8,128)(2,1)} %get-tuple-element.142) | copy-start | bytes 3145732
  520.4 7.4 %copy-start.7 = (f32[32,128]{1,0:T(8,128)S(1)}, f32[32,128]{1,0:T(8,128)}, u32[]{:S(2)}) copy-start(f32[32,128]{1,0:T(8,128)} %param.14) | copy-start | bytes 49156
  527.8 3.7 copy-start.1
Sparse Core Ops, SparseCore 0:
  10.8 60.1 all-gather.5
  73.7 59.5 all-gather.7
  136.2 349.7 all-gather.9
where the time goes:
time: 542 us; the launch traced here: 538 us
  waiting for transfers between devices  379 us (70%)
  other arithmetic  59.3 us (11%)
  matrix products  43.7 us (8%)
  blocking collectives  31.6 us (6%)
  between operations  14.4 us (3%)
  local copies, waits for them, and re-layouts  9.23 us (2%)
    all_gather x1, waiting for transfers between devices, carried_in(): everything = jax.tree.map(lambda part: lax.all_gather(part, axis), x)  336 us
    select_n x16, other arithmetic, hop(): return jax.tree.map(lambda a, b: jnp.where(reached, a, b), new, before)  33.6 us
    all_gather x1, waiting for transfers between devices, softmax_part(): value_piece = lax.all_gather(attn_value, 'ctx', axis=0, tiled=True)  30.7 us
    unnamed x1, blocking collectives  29 us
    dot_general x1, matrix products, attend(): jnp.einsum('gqd,pgd->gqp', group_query, key_piece, preferred_element_type...  16.4 us
    reduce_sum x1, other arithmetic, attend(): totals = jnp.sum(prob_rows, axis=2)  15.3 us
    dot_general x1, matrix products, attend(): jnp.einsum('gqp,pgd->gqd', prob_rows.astype(jnp.bfloat16), value_piece, p...  15.1 us
    all_gather x1, waiting for transfers between devices, softmax_part(): key_piece = lax.all_gather(attn_key, 'ctx', axis=0, tiled=True)  11.9 us
  transfers between devices with their start and end apart: 3, of which 3 were waited for; matrix products, arithmetic and copies ran while one was open for 12% of the time, Pallas kernels for 0%

commit v1 on v0

v1 whole, which is shorter than its diff:
```python
import functools
import math

import jax
import jax.numpy as jnp
from jax import lax
from jax.experimental import pallas as pl
from jax.experimental.pallas import tpu as pltpu
from jax.sharding import PartitionSpec as P

QUERY_HEADS = 64
HD = 128
GROUP = 4
F32 = jnp.float32
BF16 = jnp.bfloat16
MESH = pl.DeviceIdType.MESH
NT = (((1,), (1,)), ((), ()))
TN = (((0,), (0,)), ((), ()))
MQ = 256


def silu(x):
    return x / (1.0 + jnp.exp(-x))


def kernel(
    planes, heads_dev, lq, lk, lv, decay, gain, aq, kv_in, lin_out, attn_out,
    qf, kf, vf, mixed, kv, qs, acc, m_ref, l_ref, ot, cum_ref, lastb,
    sbuf, rs, prior, pr_send, carry, carry_out, rowsq, rowsq_in,
    z_s, z_r, x_s, x_r, y_s, y_r, dk_s, dk_r, dv_s, dv_r,
    s1_s, s1_r, la_s, la_r, s3_s, s3_r, c_s, c_r, h_s, h_r,
):
    rows, heads, _ = lq.shape
    kv_local = kv_in.shape[1]
    group = heads // kv_local
    quarter = heads // GROUP
    me = lax.axis_index("ctx")
    my_head = lax.axis_index("head")
    z = me // GROUP
    p = me % GROUP
    base = z * GROUP
    px = jnp.where(p % 2 == 0, p + 1, p - 1)
    py = (p + 2) % GROUP
    pd = jnp.where(px >= 2, px - 2, px + 2)
    peers = (px, py, pd)
    has_up = z < planes - 1
    has_down = z > 0

    def remote(src, dst, s, r, ctx):
        return pltpu.make_async_remote_copy(
            src_ref=src, dst_ref=dst, send_sem=s, recv_sem=r,
            device_id={"ctx": ctx}, device_id_type=MESH,
        )

    kv[:, :, z, p] = kv_in[...]

    barrier = pltpu.get_barrier_semaphore()
    for peer in peers:
        pl.semaphore_signal(barrier, inc=1, device_id={"ctx": base + peer}, device_id_type=MESH)
    for j in range(1, heads_dev):
        pl.semaphore_signal(
            barrier, inc=1, device_id={"head": (my_head + j) % heads_dev}, device_id_type=MESH
        )

    @pl.when(has_up)
    def _():
        pl.semaphore_signal(barrier, inc=1, device_id={"ctx": me + GROUP}, device_id_type=MESH)

    @pl.when(has_down)
    def _():
        pl.semaphore_signal(barrier, inc=1, device_id={"ctx": me - GROUP}, device_id_type=MESH)

    along = jnp.where(has_up, 1, 0) + jnp.where(has_down, 1, 0)
    pl.semaphore_wait(barrier, GROUP - 1 + heads_dev - 1 + along)

    def block(zz, col):
        return kv.at[:, :, zz, col]

    def up_copy(zz):
        return remote(block(zz, p), block(zz, p), z_s.at[zz], z_r.at[zz], me + GROUP)

    def x_copy(zz, col):
        return remote(block(zz, col), block(zz, col), x_s.at[zz], x_r.at[zz], base + px)

    def y_copy(zz, col):
        return remote(block(zz, col), block(zz, col), y_s.at[zz], y_r.at[zz], base + py)

    def dk_copy(zz, col):
        return remote(
            kv.at[0, :, zz, col], kv.at[0, :, zz, col], dk_s.at[zz], dk_r.at[zz], base + py
        )

    def dv_copy(zz, col):
        return remote(
            kv.at[1, :, zz, col], kv.at[1, :, zz, col], dv_s.at[zz], dv_r.at[zz], base + px
        )

    def send_column(zz):
        @pl.when(has_up)
        def _():
            up_copy(zz).start()

        x_copy(zz, p).start()
        y_copy(zz, p).start()

    send_column(z)

    step = 16

    def activate(src, dst):
        def body(i, _):
            t0 = pl.multiple_of(i * step, step)
            x = silu(src[pl.ds(t0, step)].astype(F32))
            r0 = pl.multiple_of(t0 * heads, step * heads)
            dst[pl.ds(r0, step * heads), :] = x.reshape(step * heads, HD)
            return 0

        lax.fori_loop(0, rows // step, body, 0)

    def head_rows(ref, h):
        return ref[pl.ds(h, rows, stride=heads), :]

    row_id = lax.broadcasted_iota(jnp.int32, (rows, rows), 0)
    col_id = lax.broadcasted_iota(jnp.int32, (rows, rows), 1)
    upper = jnp.where(row_id <= col_id, 1.0, 0.0).astype(F32)
    cum_all = lax.dot_general(
        decay[...], upper, (((1,), (0,)), ((), ())),
        precision=lax.Precision.HIGHEST, preferred_element_type=F32,
    )
    cum_ref[...] = cum_all
    lastb[p] = jnp.broadcast_to(cum_all[:, rows - 1 : rows], (heads, HD))
    last_copies = [
        remote(lastb.at[p], lastb.at[p], la_s.at[i], la_r.at[i], base + peer)
        for i, peer in enumerate(peers)
    ]
    for c in last_copies:
        c.start()

    activate(lk, kf)
    activate(lv, vf)

    def cum_of(h):
        row = jnp.broadcast_to(cum_ref[pl.ds(h, 1), :], (rows, rows))
        return row, row.T

    def local_state(h, _):
        row, col = cum_of(h)
        last = jnp.broadcast_to(lastb[p, pl.ds(h, 1), :], (rows, HD))
        sk = (head_rows(kf, h).astype(BF16).astype(F32) * jnp.exp(last - col)).astype(BF16)
        v = head_rows(vf, h).astype(BF16)
        st = lax.dot_general(sk, v, TN, preferred_element_type=F32)
        sbuf[h // quarter, h % quarter] = st.astype(BF16)
        return 0

    lax.fori_loop(0, heads, local_state, 0)

    s1 = [
        remote(sbuf.at[peer], rs.at[p], s1_s.at[i], s1_r.at[i], base + peer)
        for i, peer in enumerate(peers)
    ]
    for c in s1:
        c.start()

    def load_queries(i, _):
        t0 = pl.multiple_of(i * step, step)
        x = aq[pl.ds(t0, step)].astype(F32)
        for g in range(kv_local):
            part = x[:, g * group : (g + 1) * group, :].reshape(step * group, HD)
            r0 = pl.multiple_of(t0 * group, step * group)
            qs[g, pl.ds(r0, step * group), :] = part.astype(BF16)
        return 0

    lax.fori_loop(0, rows // step, load_queries, 0)
    activate(lq, qf)

    def inner(h, _):
        row, col = cum_of(h)
        q = head_rows(qf, h).astype(BF16)
        k = head_rows(kf, h).astype(BF16)
        v = head_rows(vf, h).astype(BF16)
        sc = lax.dot_general(q, k, NT, preferred_element_type=F32)
        dm = jnp.exp(jnp.where(row_id >= col_id, col - row, -1e30))
        w = (sc * dm).astype(BF16)
        mixed[pl.ds(h, rows, stride=heads), :] = jnp.dot(w, v, preferred_element_type=F32)
        return 0

    lax.fori_loop(0, heads, inner, 0)

    m_ref[...] = jnp.full(m_ref.shape, -1e30, F32)
    l_ref[...] = jnp.zeros(l_ref.shape, F32)
    acc[...] = jnp.zeros(acc.shape, F32)
    scale = HD ** (-0.5) * math.log2(math.e)
    span = GROUP * rows
    tiles = rows * group // MQ

    def attend(zz, masked):
        def body(i, _):
            g = i // tiles
            q0 = pl.multiple_of((i % tiles) * MQ, MQ)
            cols = pl.ds(q0, MQ)
            k = kv[0, g, zz].reshape(span, HD)
            v = kv[1, g, zz].reshape(span, HD)
            s = lax.dot_general(k, qs[g, cols, :], NT, preferred_element_type=F32) * scale
            if masked:
                key_pos = lax.broadcasted_iota(jnp.int32, (span, MQ), 0)
                q_pos = p * rows + (q0 + lax.broadcasted_iota(jnp.int32, (span, MQ), 1)) // group
                s = jnp.where(key_pos <= q_pos, s, -1e30)
            m_old = m_ref[g, :, cols]
            m_new = jnp.maximum(m_old, jnp.max(s, axis=0, keepdims=True))
            alpha = jnp.exp2(m_old - m_new)
            e = jnp.exp2(s - m_new)
            m_ref[g, :, cols] = m_new
            l_ref[g, :, cols] = l_ref[g, :, cols] * alpha + jnp.sum(e, axis=0, keepdims=True)
            o = lax.dot_general(v, e.astype(BF16), TN, preferred_element_type=F32)
            acc[g, :, cols] = acc[g, :, cols] * alpha + o
            return 0

        lax.fori_loop(0, kv_local * tiles, body, 0)

    def carry_copy():
        return remote(carry_out, carry, c_s, c_r, me + GROUP)

    def state_chain():
        for i in range(GROUP - 1):
            s1[i].wait_recv()
            last_copies[i].wait_recv()
        rs[p] = sbuf[p]

        @pl.when(has_down)
        def _():
            carry_copy().wait_recv()

        @pl.when(jnp.logical_not(has_down))
        def _():
            carry[...] = jnp.zeros(carry.shape, BF16)

        def one(hh, _):
            h = p * quarter + hh
            state = carry[hh].astype(F32)
            for i in range(GROUP):
                pr_send[i, hh] = state.astype(BF16)
                d = jnp.exp(lastb[i, pl.ds(h, 1), :])
                state = d * state + rs[i, hh].astype(F32)
            carry_out[hh] = state.astype(BF16)
            return 0

        lax.fori_loop(0, quarter, one, 0)

        @pl.when(has_up)
        def _():
            carry_copy().start()

        for c in s3:
            c.start()
        prior[p] = pr_send[p]

    s3 = [
        remote(pr_send.at[peer], prior.at[p], s3_s.at[i], s3_r.at[i], base + peer)
        for i, peer in enumerate(peers)
    ]

    def turn(r, _):
        zz = z - r

        @pl.when(r < z)
        def _():
            up_copy(zz - 1).wait_recv()
            send_column(zz - 1)

        @pl.when(r <= z)
        def _():
            x_copy(zz, px).wait_recv()
            dk_copy(zz, px).start()
            y_copy(zz, py).wait_recv()
            dv_copy(zz, py).start()

        @pl.when(r == z + 1)
        def _():
            state_chain()

        @pl.when(r > 0)
        def _():
            dk_copy(zz + 1, pd).wait_recv()
            dv_copy(zz + 1, pd).wait_recv()

        @pl.when(r == 1)
        def _():
            attend(zz + 1, True)

        @pl.when(r > 1)
        def _():
            attend(zz + 1, False)

        return 0

    lax.fori_loop(0, z + 2, turn, 0)

    for c in s3:
        c.wait_recv()
    rowsq[...] = jnp.zeros(rowsq.shape, F32)

    def outer(h, _):
        _, col = cum_of(h)
        q = head_rows(qf, h).astype(BF16)
        o = jnp.dot(q, prior[h // quarter, h % quarter], preferred_element_type=F32)
        mx = head_rows(mixed, h) + o * jnp.exp(col)
        mixed[pl.ds(h, rows, stride=heads), :] = mx
        rowsq[...] += mx * mx
        return 0

    lax.fori_loop(0, heads, outer, 0)
    h_copies = [
        pltpu.make_async_remote_copy(
            src_ref=rowsq, dst_ref=rowsq_in.at[j - 1], send_sem=h_s.at[j - 1],
            recv_sem=h_r.at[j - 1], device_id={"head": (my_head + j) % heads_dev},
            device_id_type=MESH,
        )
        for j in range(1, heads_dev)
    ]
    for c in h_copies:
        c.start()

    for g in range(kv_local):
        for t in range(tiles):
            cols = slice(t * MQ, (t + 1) * MQ)
            ot[g, cols, :] = (acc[g, :, cols] / l_ref[g, :, cols]).T

    def store_attn(i, _):
        t0 = pl.multiple_of(i * step, step)
        r0 = pl.multiple_of(t0 * group, step * group)
        parts = [
            ot[g, pl.ds(r0, step * group), :].reshape(step, group, HD) for g in range(kv_local)
        ]
        attn_out[pl.ds(t0, step)] = jnp.concatenate(parts, axis=1).astype(BF16)
        return 0

    lax.fori_loop(0, rows // step, store_attn, 0)

    for c in h_copies:
        c.wait_recv()
    total = rowsq[...]
    for j in range(heads_dev - 1):
        total = total + rowsq_in[j]
    mean = jnp.sum(total, axis=1, keepdims=True) / (heads_dev * heads * HD)
    for c in h_copies:
        c.wait_send()
    rowsq[...] = jnp.broadcast_to(lax.rsqrt(mean + 1e-06), (rows, HD))

    def store_lin(i, _):
        t0 = pl.multiple_of(i * step, step)
        r0 = pl.multiple_of(t0 * heads, step * heads)
        x = mixed[pl.ds(r0, step * heads), :].reshape(step, heads, HD)
        inv = rowsq[pl.ds(t0, step), :].reshape(step, 1, HD)
        lin_out[pl.ds(t0, step)] = (x * inv * gain[...][None]).astype(BF16)
        return 0

    lax.fori_loop(0, rows // step, store_lin, 0)

    for c in last_copies + s1 + s3:
        c.wait_send()

    @pl.when(has_up)
    def _():
        carry_copy().wait_send()

    def drain(zz, _):
        @pl.when(has_up)
        def _():
            up_copy(zz).wait_send()

        x_copy(zz, p).wait_send()
        y_copy(zz, p).wait_send()
        dk_copy(zz, px).wait_send()
        dv_copy(zz, py).wait_send()
        return 0

    lax.fori_loop(0, z + 1, drain, 0)


def local(planes, heads_dev, lin_query, lin_key, lin_value, log_decay, norm_gain,
          attn_query, attn_key, attn_value):
    rows, heads, _ = lin_query.shape
    kv_local = attn_key.shape[1]
    group = heads // kv_local
    quarter = heads // GROUP
    kv_in = jnp.stack([attn_key.transpose(1, 0, 2), attn_value.transpose(1, 0, 2)])
    vmem = pl.BlockSpec(memory_space=pltpu.VMEM)
    dma = pltpu.SemaphoreType.DMA
    out = jax.ShapeDtypeStruct(lin_query.shape, BF16)
    state = (GROUP, quarter, HD, HD)
    return pl.pallas_call(
        functools.partial(kernel, planes, heads_dev),
        out_shape=(out, out),
        in_specs=[vmem] * 7,
        out_specs=(vmem, vmem),
        scratch_shapes=[
            pltpu.VMEM((rows * heads, HD), F32),
            pltpu.VMEM((rows * heads, HD), F32),
            pltpu.VMEM((rows * heads, HD), F32),
            pltpu.VMEM((rows * heads, HD), F32),
            pltpu.VMEM((2, kv_local, planes, GROUP, rows, HD), BF16),
            pltpu.VMEM((kv_local, rows * group, HD), BF16),
            pltpu.VMEM((kv_local, HD, rows * group), F32),
            pltpu.VMEM((kv_local, 1, rows * group), F32),
            pltpu.VMEM((kv_local, 1, rows * group), F32),
            pltpu.VMEM((kv_local, rows * group, HD), F32),
            pltpu.VMEM((heads, rows), F32),
            pltpu.VMEM((GROUP, heads, HD), F32),
            pltpu.VMEM(state, BF16),
            pltpu.VMEM(state, BF16),
            pltpu.VMEM(state, BF16),
            pltpu.VMEM(state, BF16),
            pltpu.VMEM(state[1:], BF16),
            pltpu.VMEM(state[1:], BF16),
            pltpu.VMEM((rows, HD), F32),
            pltpu.VMEM((max(heads_dev - 1, 1), rows, HD), F32),
        ]
        + [dma((planes,))] * 10
        + [dma((GROUP - 1,))] * 6
        + [dma, dma]
        + [dma((max(heads_dev - 1, 1),))] * 2,
        compiler_params=pltpu.CompilerParams(
            collective_id=0, has_side_effects=True, vmem_limit_bytes=56 * 2**20
        ),
        name="mixers",
    )(lin_query, lin_key, lin_value, log_decay, norm_gain, attn_query, kv_in)


def solution(mesh):
    planes = mesh.shape["ctx"] // GROUP
    return jax.shard_map(
        functools.partial(local, planes, mesh.shape["head"]),
        mesh=mesh,
        in_specs=(
            P("ctx", "head", None),
            P("ctx", "head", None),
            P("ctx", "head", None),
            P("head", "ctx"),
            P("head", None),
            P("ctx", "head", None),
            P("ctx", "head", None),
            P("ctx", "head", None),
        ),
        out_specs=(P("ctx", "head", None), P("ctx", "head", None)),
        check_vma=False,
    )
```

time: 542 us -> 94.6 us (0.17)
  waiting for transfers between devices: 379 us -> 0 us
  Pallas kernels: 0 us -> 88.6 us
  other arithmetic: 59.3 us -> 0.73 us
  matrix products: 43.7 us -> 0 us
  blocking collectives: 31.6 us -> 0 us
  between operations: 14.4 us -> 0.65 us
    all_gather x3 -> x0, waiting for transfers between devices: 379 us -> none  [the longest x1 336 us: carried_in(): everything = jax.tree.map(lambda part: lax.all_gather(part, axis), x)]
    pallas_call x0 -> x1, Pallas kernels: none -> 88.6 us  [local(): pl.pallas_call(functools.partial(kernel, planes, heads_dev), out_shape=(o...]
    dot_general x5 -> x0, matrix products: 43.7 us -> none  [the longest x1 16.4 us: attend(): jnp.einsum('gqd,pgd->gqp', group_query, key_piece, preferred_element_type...]
    select_n x16 -> x0, other arithmetic: 33.6 us -> none  [hop(): return jax.tree.map(lambda a, b: jnp.where(reached, a, b), new, before)]
    unnamed x1 -> x0, blocking collectives: 29 us -> none
    reduce_sum x1 -> x0, other arithmetic: 15.3 us -> none  [attend(): totals = jnp.sum(prob_rows, axis=2)]
    convert_element_type x3 -> x0, other arithmetic: 6.66 us -> none  [the longest x1 2.58 us: lightning(): (act_key.astype(jnp.float32) * key_factor[:, :, None]).astype(jnp.bfloat16)]
  transfers between devices with their start and end apart: 3 -> 0, of which waited for: 3 -> 0; matrix products, arithmetic and copies ran while one was open for 12% -> 0% of each run, Pallas kernels for 0% -> 0%
where the time goes in v1:
time: 94.6 us; the launch traced here: 94.3 us
  Pallas kernels  88.6 us (94%)
  local copies, waits for them, and re-layouts  4.33 us (5%)
    pallas_call x1, Pallas kernels, local(): pl.pallas_call(functools.partial(kernel, planes, heads_dev), out_shape=(o...  88.6 us
    unnamed x4, local copies, waits for them, and re-layouts  3.32 us

profile of v1, /device:TPU:29, one launch (start us, length us, event | category | flops | bytes accessed | tf_op | source)
XLA Modules:
  0.0 94.3 jit_solution(8785927341393720089)
XLA Ops:
  0.6 1.0 %copy_bitcast_fusion = (bf16[1,4,128,128]{3,2,1,0:T(8,128)(2,1)S(1)}, bf16[1,4,128,128]{3,2,1,0:T(8,128)(2,1)S(1)}) fusion(bf16[128,4,128]{2,1,0:T(4,128)(2,1)} %param.15, bf16[128,4,128]{2,1,0:T(4,128)(2,1)} %param.14), kind=kLoop, calls=%fused_computation.1 | loop fusion | bytes 524288 | tf_op jit(solution)/shard_map/stack | solution.py:386
  1.6 0.7 pad_maximum_fusion.kv_in
  2.4 88.6 %mixers.1 = (bf16[128,32,128]{2,1,0:T(8,128)(2,1)}, bf16[128,32,128]{2,1,0:T(8,128)(2,1)}) custom-call(bf16[128,32,128]{2,1,0:T(8,128)(2,1)} %lq.1, bf16[128,32,128]{2,1,0:T(8,128)(2,1)} %lk.1, bf16[128,32,128]{2,1,0:T(8,128)(2,1)} %lv.1, f32[32,128]{1,0:T(8,128)} %decay.1, f32[32,128]{1,0:T(8,128)} %gain.1, bf16[128,32,128]{2,1,0:T(8,128)(2,1)} %aq.1, ...), custom_call_target="tpu_custom_call" | custom-call | tf_op jit(solution)/shard_map/mixers/pallas_call | solution.py:391
  91.0 0.0 copy-start
  91.0 2.4 %copy.16 = bf16[128,32,128]{2,1,0:T(8,128)(2,1)} copy(bf16[128,32,128]{2,1,0:T(8,128)(2,1)} %get-tuple-element.6) | data formatting | bytes 2097152
  93.4 0.0 copy-done
  93.4 1.0 %copy.17 = bf16[128,32,128]{2,1,0:T(8,128)(2,1)} copy(bf16[128,32,128]{2,1,0:T(8,128)(2,1)S(1)} %copy-done) | data formatting | bytes 2097152
Async XLA Ops:
  91.0 2.4 %copy-start = (bf16[128,32,128]{2,1,0:T(8,128)(2,1)S(1)}, bf16[128,32,128]{2,1,0:T(8,128)(2,1)}, u32[]{:S(2)}) copy-start(bf16[128,32,128]{2,1,0:T(8,128)(2,1)} %get-tuple-element.7) | copy-start | bytes 3145732

commit v2 on v1

--- a/solution.py
+++ b/solution.py
@@ -17,21 +17,23 @@
 NT = (((1,), (1,)), ((), ()))
 TN = (((0,), (0,)), ((), ()))
 MQ = 256
+PARTS = 2
 
 
 def silu(x):
-    return x / (1.0 + jnp.exp(-x))
+    half = 0.5 * x
+    return half + half * jnp.tanh(half)
 
 
 def kernel(
-    planes, heads_dev, lq, lk, lv, decay, gain, aq, kv_in, lin_out, attn_out,
-    qf, kf, vf, mixed, kv, qs, acc, m_ref, l_ref, ot, cum_ref, lastb,
+    planes, heads_dev, lq, lk, lv, decay, gain, aq, k_in, v_in, lin_out, attn_out,
+    qf, kf, vf, mixed, kv, qs, acc, m_ref, l_ref, ot, cum_ref, colb, lastb,
     sbuf, rs, prior, pr_send, carry, carry_out, rowsq, rowsq_in,
     z_s, z_r, x_s, x_r, y_s, y_r, dk_s, dk_r, dv_s, dv_r,
     s1_s, s1_r, la_s, la_r, s3_s, s3_r, c_s, c_r, h_s, h_r,
 ):
     rows, heads, _ = lq.shape
-    kv_local = kv_in.shape[1]
+    kv_local = k_in.shape[0]
     group = heads // kv_local
     quarter = heads // GROUP
     me = lax.axis_index("ctx")
@@ -52,7 +54,8 @@
             device_id={"ctx": ctx}, device_id_type=MESH,
         )
 
-    kv[:, :, z, p] = kv_in[...]
+    kv[0, :, z, p] = k_in[...]
+    kv[1, :, z, p] = v_in[...]
 
     barrier = pltpu.get_barrier_semaphore()
     for peer in peers:
@@ -139,27 +142,39 @@
     activate(lk, kf)
     activate(lv, vf)
 
-    def cum_of(h):
-        row = jnp.broadcast_to(cum_ref[pl.ds(h, 1), :], (rows, rows))
-        return row, row.T
-
-    def local_state(h, _):
-        row, col = cum_of(h)
-        last = jnp.broadcast_to(lastb[p, pl.ds(h, 1), :], (rows, HD))
-        sk = (head_rows(kf, h).astype(BF16).astype(F32) * jnp.exp(last - col)).astype(BF16)
-        v = head_rows(vf, h).astype(BF16)
-        st = lax.dot_general(sk, v, TN, preferred_element_type=F32)
-        sbuf[h // quarter, h % quarter] = st.astype(BF16)
-        return 0
-
-    lax.fori_loop(0, heads, local_state, 0)
+    together = min(4, quarter)
+
+    def cum_row(h):
+        return jnp.broadcast_to(cum_ref[pl.ds(h, 1), :], (rows, rows))
+
+    def local_states(owner):
+        def body(i, _):
+            hs = [i * together + u for u in range(together)]
+            ids = [owner * quarter + hh for hh in hs]
+            ks = [head_rows(kf, h).astype(BF16).astype(F32) for h in ids]
+            vs = [head_rows(vf, h).astype(BF16) for h in ids]
+            lasts = [jnp.broadcast_to(lastb[p, pl.ds(h, 1), :], (rows, HD)) for h in ids]
+            cols = [cum_row(h).T for h in ids]
+            sks = [(k * jnp.exp(a - c)).astype(BF16) for k, a, c in zip(ks, lasts, cols)]
+            sts = [
+                lax.dot_general(sk, v, TN, preferred_element_type=F32) for sk, v in zip(sks, vs)
+            ]
+            for h, c in zip(ids, cols):
+                colb[h] = c
+            for hh, st in zip(hs, sts):
+                sbuf[owner, hh] = st.astype(BF16)
+            return 0
+
+        lax.fori_loop(0, quarter // together, body, 0)
 
     s1 = [
         remote(sbuf.at[peer], rs.at[p], s1_s.at[i], s1_r.at[i], base + peer)
         for i, peer in enumerate(peers)
     ]
-    for c in s1:
+    for peer, c in zip(peers, s1):
+        local_states(peer)
         c.start()
+    local_states(p)
 
     def load_queries(i, _):
         t0 = pl.multiple_of(i * step, step)
@@ -173,18 +188,21 @@
     lax.fori_loop(0, rows // step, load_queries, 0)
     activate(lq, qf)
 
-    def inner(h, _):
-        row, col = cum_of(h)
-        q = head_rows(qf, h).astype(BF16)
-        k = head_rows(kf, h).astype(BF16)
-        v = head_rows(vf, h).astype(BF16)
-        sc = lax.dot_general(q, k, NT, preferred_element_type=F32)
-        dm = jnp.exp(jnp.where(row_id >= col_id, col - row, -1e30))
-        w = (sc * dm).astype(BF16)
-        mixed[pl.ds(h, rows, stride=heads), :] = jnp.dot(w, v, preferred_element_type=F32)
-        return 0
-
-    lax.fori_loop(0, heads, inner, 0)
+    def inner(i, _):
+        ids = [i * together + u for u in range(together)]
+        qh = [head_rows(qf, h).astype(BF16) for h in ids]
+        ks = [head_rows(kf, h).astype(BF16) for h in ids]
+        vs = [head_rows(vf, h).astype(BF16) for h in ids]
+        spread = [colb[h] - cum_row(h) for h in ids]
+        sc = [lax.dot_general(q, k, NT, preferred_element_type=F32) for q, k in zip(qh, ks)]
+        dm = [jnp.exp(jnp.where(row_id >= col_id, d, -1e30)) for d in spread]
+        ws = [(a * d).astype(BF16) for a, d in zip(sc, dm)]
+        outs = [jnp.dot(w, v, preferred_element_type=F32) for w, v in zip(ws, vs)]
+        for h, o in zip(ids, outs):
+            mixed[pl.ds(h, rows, stride=heads), :] = o
+        return 0
+
+    lax.fori_loop(0, heads // together, inner, 0)
 
     m_ref[...] = jnp.full(m_ref.shape, -1e30, F32)
     l_ref[...] = jnp.zeros(l_ref.shape, F32)
@@ -193,32 +211,62 @@
     span = GROUP * rows
     tiles = rows * group // MQ
 
+    pair = 2
+    sets = tiles // pair
+
     def attend(zz, masked):
         def body(i, _):
-            g = i // tiles
-            q0 = pl.multiple_of((i % tiles) * MQ, MQ)
-            cols = pl.ds(q0, MQ)
+            g = i // sets
+            starts = [pl.multiple_of(((i % sets) * pair + u) * MQ, MQ) for u in range(pair)]
+            cols = [pl.ds(q0, MQ) for q0 in starts]
             k = kv[0, g, zz].reshape(span, HD)
             v = kv[1, g, zz].reshape(span, HD)
-            s = lax.dot_general(k, qs[g, cols, :], NT, preferred_element_type=F32) * scale
+            ss = [
+                lax.dot_general(k, qs[g, c, :], NT, preferred_element_type=F32) * scale
+                for c in cols
+            ]
             if masked:
                 key_pos = lax.broadcasted_iota(jnp.int32, (span, MQ), 0)
-                q_pos = p * rows + (q0 + lax.broadcasted_iota(jnp.int32, (span, MQ), 1)) // group
-                s = jnp.where(key_pos <= q_pos, s, -1e30)
-            m_old = m_ref[g, :, cols]
-            m_new = jnp.maximum(m_old, jnp.max(s, axis=0, keepdims=True))
-            alpha = jnp.exp2(m_old - m_new)
-            e = jnp.exp2(s - m_new)
-            m_ref[g, :, cols] = m_new
-            l_ref[g, :, cols] = l_ref[g, :, cols] * alpha + jnp.sum(e, axis=0, keepdims=True)
-            o = lax.dot_general(v, e.astype(BF16), TN, preferred_element_type=F32)
-            acc[g, :, cols] = acc[g, :, cols] * alpha + o
+                col_pos = lax.broadcasted_iota(jnp.int32, (span, MQ), 1)
+                ss = [
+                    jnp.where(key_pos <= p * rows + (q0 + col_pos) // group, x, -1e30)
+                    for q0, x in zip(starts, ss)
+                ]
+            m_old = [m_ref[g, :, c] for c in cols]
+            l_old = [l_ref[g, :, c] for c in cols]
+            a_old = [acc[g, :, c] for c in cols]
+            m_new = [
+                jnp.maximum(m, jnp.max(x, axis=0, keepdims=True)) for m, x in zip(m_old, ss)
+            ]
+            alpha = [jnp.exp2(a - b) for a, b in zip(m_old, m_new)]
+            es = [jnp.exp2(x - m) for x, m in zip(ss, m_new)]
+            l_new = [
+                old * a + jnp.sum(e, axis=0, keepdims=True)
+                for old, a, e in zip(l_old, alpha, es)
+            ]
+            os = [
+                lax.dot_general(v, e.astype(BF16), TN, preferred_element_type=F32) for e in es
+            ]
+            for u, c in enumerate(cols):
+                m_ref[g, :, c] = m_new[u]
+                l_ref[g, :, c] = l_new[u]
+                acc[g, :, c] = a_old[u] * alpha[u] + os[u]
             return 0
 
-        lax.fori_loop(0, kv_local * tiles, body, 0)
-
-    def carry_copy():
-        return remote(carry_out, carry, c_s, c_r, me + GROUP)
+        lax.fori_loop(0, kv_local * sets, body, 0)
+
+    part = quarter // PARTS
+
+    def carry_copy(j):
+        own = pl.ds(j * part, part)
+        return remote(carry_out.at[own], carry.at[own], c_s.at[j], c_r.at[j], me + GROUP)
+
+    def prior_copy(j, i):
+        own = pl.ds(j * part, part)
+        n = j * (GROUP - 1) + i
+        return remote(
+            pr_send.at[peers[i], own], prior.at[p, own], s3_s.at[n], s3_r.at[n], base + peers[i]
+        )
 
     def state_chain():
         for i in range(GROUP - 1):
@@ -226,38 +274,36 @@
             last_copies[i].wait_recv()
         rs[p] = sbuf[p]
 
-        @pl.when(has_down)
-        def _():
-            carry_copy().wait_recv()
-
         @pl.when(jnp.logical_not(has_down))
         def _():
             carry[...] = jnp.zeros(carry.shape, BF16)
 
-        def one(hh, _):
-            h = p * quarter + hh
-            state = carry[hh].astype(F32)
-            for i in range(GROUP):
-                pr_send[i, hh] = state.astype(BF16)
-                d = jnp.exp(lastb[i, pl.ds(h, 1), :])
-                state = d * state + rs[i, hh].astype(F32)
-            carry_out[hh] = state.astype(BF16)
-            return 0
-
-        lax.fori_loop(0, quarter, one, 0)
-
-        @pl.when(has_up)
-        def _():
-            carry_copy().start()
-
-        for c in s3:
-            c.start()
+        for j in range(PARTS):
+
+            @pl.when(has_down)
+            def _():
+                carry_copy(j).wait_recv()
+
+            def one(n, _):
+                hh = j * part + n
+                h = p * quarter + hh
+                state = carry[hh].astype(F32)
+                for i in range(GROUP):
+                    pr_send[i, hh] = state.astype(BF16)
+                    d = jnp.exp(lastb[i, pl.ds(h, 1), :])
+                    state = d * state + rs[i, hh].astype(F32)
+                carry_out[hh] = state.astype(BF16)
+                return 0
+
+            lax.fori_loop(0, part, one, 0)
+
+            @pl.when(has_up)
+            def _():
+                carry_copy(j).start()
+
+            for i in range(GROUP - 1):
+                prior_copy(j, i).start()
         prior[p] = pr_send[p]
-
-    s3 = [
-        remote(pr_send.at[peer], prior.at[p], s3_s.at[i], s3_r.at[i], base + peer)
-        for i, peer in enumerate(peers)
-    ]
 
     def turn(r, _):
         zz = z - r
@@ -295,20 +341,40 @@
 
     lax.fori_loop(0, z + 2, turn, 0)
 
-    for c in s3:
-        c.wait_recv()
+    for g in range(kv_local):
+        for t in range(tiles):
+            cols = slice(t * MQ, (t + 1) * MQ)
+            ot[g, cols, :] = (acc[g, :, cols] / l_ref[g, :, cols]).T
+
+    def store_attn(i, _):
+        t0 = pl.multiple_of(i * step, step)
+        r0 = pl.multiple_of(t0 * group, step * group)
+        parts = [
+            ot[g, pl.ds(r0, step * group), :].reshape(step, group, HD) for g in range(kv_local)
+        ]
+        attn_out[pl.ds(t0, step)] = jnp.concatenate(parts, axis=1).astype(BF16)
+        return 0
+
+    lax.fori_loop(0, rows // step, store_attn, 0)
+
+    for j in range(PARTS):
+        for i in range(GROUP - 1):
+            prior_copy(j, i).wait_recv()
     rowsq[...] = jnp.zeros(rowsq.shape, F32)
 
-    def outer(h, _):
-        _, col = cum_of(h)
-        q = head_rows(qf, h).astype(BF16)
-        o = jnp.dot(q, prior[h // quarter, h % quarter], preferred_element_type=F32)
-        mx = head_rows(mixed, h) + o * jnp.exp(col)
-        mixed[pl.ds(h, rows, stride=heads), :] = mx
-        rowsq[...] += mx * mx
-        return 0
-
-    lax.fori_loop(0, heads, outer, 0)
+    def outer(i, _):
+        ids = [i * together + u for u in range(together)]
+        qh = [head_rows(qf, h).astype(BF16) for h in ids]
+        old = [head_rows(mixed, h) for h in ids]
+        ps = [prior[h // quarter, h % quarter] for h in ids]
+        os = [jnp.dot(q, x, preferred_element_type=F32) for q, x in zip(qh, ps)]
+        new = [a + o * jnp.exp(colb[h]) for a, o, h in zip(old, os, ids)]
+        for h, x in zip(ids, new):
+            mixed[pl.ds(h, rows, stride=heads), :] = x
+        rowsq[...] += sum(x * x for x in new)
+        return 0
+
+    lax.fori_loop(0, heads // together, outer, 0)
     h_copies = [
         pltpu.make_async_remote_copy(
             src_ref=rowsq, dst_ref=rowsq_in.at[j - 1], send_sem=h_s.at[j - 1],
@@ -320,22 +386,6 @@
     for c in h_copies:
         c.start()
 
-    for g in range(kv_local):
-        for t in range(tiles):
-            cols = slice(t * MQ, (t + 1) * MQ)
-            ot[g, cols, :] = (acc[g, :, cols] / l_ref[g, :, cols]).T
-
-    def store_attn(i, _):
-        t0 = pl.multiple_of(i * step, step)
-        r0 = pl.multiple_of(t0 * group, step * group)
-        parts = [
-            ot[g, pl.ds(r0, step * group), :].reshape(step, group, HD) for g in range(kv_local)
-        ]
-        attn_out[pl.ds(t0, step)] = jnp.concatenate(parts, axis=1).astype(BF16)
-        return 0
-
-    lax.fori_loop(0, rows // step, store_attn, 0)
-
     for c in h_copies:
         c.wait_recv()
     total = rowsq[...]
@@ -356,12 +406,16 @@
 
     lax.fori_loop(0, rows // step, store_lin, 0)
 
-    for c in last_copies + s1 + s3:
+    for c in last_copies + s1:
         c.wait_send()
+    for j in range(PARTS):
+        for i in range(GROUP - 1):
+            prior_copy(j, i).wait_send()
 
     @pl.when(has_up)
     def _():
-        carry_copy().wait_send()
+        for j in range(PARTS):
+            carry_copy(j).wait_send()
 
     def drain(zz, _):
         @pl.when(has_up)
@@ -383,7 +437,6 @@
     kv_local = attn_key.shape[1]
     group = heads // kv_local
     quarter = heads // GROUP
-    kv_in = jnp.stack([attn_key.transpose(1, 0, 2), attn_value.transpose(1, 0, 2)])
     vmem = pl.BlockSpec(memory_space=pltpu.VMEM)
     dma = pltpu.SemaphoreType.DMA
     out = jax.ShapeDtypeStruct(lin_query.shape, BF16)
@@ -391,7 +444,7 @@
     return pl.pallas_call(
         functools.partial(kernel, planes, heads_dev),
         out_shape=(out, out),
-        in_specs=[vmem] * 7,
+        in_specs=[vmem] * 8,
         out_specs=(vmem, vmem),
         scratch_shapes=[
             pltpu.VMEM((rows * heads, HD), F32),
@@ -405,6 +458,7 @@
             pltpu.VMEM((kv_local, 1, rows * group), F32),
             pltpu.VMEM((kv_local, rows * group, HD), F32),
             pltpu.VMEM((heads, rows), F32),
+            pltpu.VMEM((heads, rows, rows), F32),
             pltpu.VMEM((GROUP, heads, HD), F32),
             pltpu.VMEM(state, BF16),
             pltpu.VMEM(state, BF16),
@@ -416,14 +470,16 @@
             pltpu.VMEM((max(heads_dev - 1, 1), rows, HD), F32),
         ]
         + [dma((planes,))] * 10
-        + [dma((GROUP - 1,))] * 6
-        + [dma, dma]
+        + [dma((GROUP - 1,))] * 4
+        + [dma(((GROUP - 1) * PARTS,))] * 2
+        + [dma((PARTS,))] * 2
         + [dma((max(heads_dev - 1, 1),))] * 2,
         compiler_params=pltpu.CompilerParams(
             collective_id=0, has_side_effects=True, vmem_limit_bytes=56 * 2**20
         ),
         name="mixers",
-    )(lin_query, lin_key, lin_value, log_decay, norm_gain, attn_query, kv_in)
+    )(lin_query, lin_key, lin_value, log_decay, norm_gain, attn_query,
+      attn_key.transpose(1, 0, 2), attn_value.transpose(1, 0, 2))
 
 
 def solution(mesh):

time: 94.6 us -> 80.5 us (0.85)
  Pallas kernels: 88.6 us -> 74.6 us
    pallas_call x1, Pallas kernels: 88.6 us -> 74.6 us  [local(): pl.pallas_call(functools.partial(kernel, planes, heads_dev), out_shape=(o...]
    transpose x0 -> x1, local copies, waits for them, and re-layouts: none -> 1.7 us  [local(): attn_value.transpose(1, 0, 2)]
    another operation x1 -> x0, local copies, waits for them, and re-layouts: 1 us -> none  [local(): jnp.stack([attn_key.transpose(1, 0, 2), attn_value.transpose(1, 0, 2)])]
where the time goes in v2:
time: 80.5 us; the launch traced here: 80.2 us
  Pallas kernels  74.6 us (93%)
  local copies, waits for them, and re-layouts  5.03 us (6%)
    pallas_call x1, Pallas kernels, local(): pl.pallas_call(functools.partial(kernel, planes, heads_dev), out_shape=(o...  74.6 us
    unnamed x4, local copies, waits for them, and re-layouts  3.32 us
    transpose x1, local copies, waits for them, and re-layouts, local(): attn_value.transpose(1, 0, 2)  1.7 us

profile of v2, /device:TPU:29, one launch (start us, length us, event | category | flops | bytes accessed | tf_op | source)
XLA Modules:
  0.0 80.2 jit_solution(15401047613754982588)
XLA Ops:
  0.6 1.7 %copy_bitcast_fusion = (bf16[4,128,128]{2,1,0:T(8,128)(2,1)}, bf16[4,128,128]{2,1,0:T(8,128)(2,1)}) fusion(bf16[128,4,128]{2,1,0:T(4,128)(2,1)} %param.15, bf16[128,4,128]{2,1,0:T(4,128)(2,1)} %param.14), kind=kLoop, calls=%fused_computation | loop fusion | bytes 524288 | tf_op jit(solution)/shard_map/transpose | solution.py:482
  2.3 74.6 %mixers.1 = (bf16[128,32,128]{2,1,0:T(8,128)(2,1)}, bf16[128,32,128]{2,1,0:T(8,128)(2,1)}) custom-call(bf16[128,32,128]{2,1,0:T(8,128)(2,1)} %lq.1, bf16[128,32,128]{2,1,0:T(8,128)(2,1)} %lk.1, bf16[128,32,128]{2,1,0:T(8,128)(2,1)} %lv.1, f32[32,128]{1,0:T(8,128)} %decay.1, f32[32,128]{1,0:T(8,128)} %gain.1, bf16[128,32,128]{2,1,0:T(8,128)(2,1)} %aq.1, ...), custom_call_target="tpu_custom_call" | custom-call | tf_op jit(solution)/shard_map/mixers/pallas_call | solution.py:444
  76.9 0.0 copy-start
  76.9 2.4 %copy.16 = bf16[128,32,128]{2,1,0:T(8,128)(2,1)} copy(bf16[128,32,128]{2,1,0:T(8,128)(2,1)} %get-tuple-element.6) | data formatting | bytes 2097152
  79.3 0.0 copy-done
  79.3 1.0 %copy.17 = bf16[128,32,128]{2,1,0:T(8,128)(2,1)} copy(bf16[128,32,128]{2,1,0:T(8,128)(2,1)S(1)} %copy-done) | data formatting | bytes 2097152
Async XLA Ops:
  76.9 2.4 %copy-start = (bf16[128,32,128]{2,1,0:T(8,128)(2,1)S(1)}, bf16[128,32,128]{2,1,0:T(8,128)(2,1)}, u32[]{:S(2)}) copy-start(bf16[128,32,128]{2,1,0:T(8,128)(2,1)} %get-tuple-element.7) | copy-start | bytes 3145732

commit v3 on v2

--- a/solution.py
+++ b/solution.py
@@ -29,7 +29,7 @@
     planes, heads_dev, lq, lk, lv, decay, gain, aq, k_in, v_in, lin_out, attn_out,
     qf, kf, vf, mixed, kv, qs, acc, m_ref, l_ref, ot, cum_ref, colb, lastb,
     sbuf, rs, prior, pr_send, carry, carry_out, rowsq, rowsq_in,
-    z_s, z_r, x_s, x_r, y_s, y_r, dk_s, dk_r, dv_s, dv_r,
+    z_s, z_r, zd_s, zd_r, x_s, x_r, y_s, y_r, dk_s, dk_r, dv_s, dv_r,
     s1_s, s1_r, la_s, la_r, s3_s, s3_r, c_s, c_r, h_s, h_r,
 ):
     rows, heads, _ = lq.shape
@@ -82,21 +82,20 @@
     def up_copy(zz):
         return remote(block(zz, p), block(zz, p), z_s.at[zz], z_r.at[zz], me + GROUP)
 
+    def up_diagonal(zz):
+        return remote(block(zz, pd), block(zz, pd), zd_s.at[zz], zd_r.at[zz], me + GROUP)
+
     def x_copy(zz, col):
         return remote(block(zz, col), block(zz, col), x_s.at[zz], x_r.at[zz], base + px)
 
     def y_copy(zz, col):
         return remote(block(zz, col), block(zz, col), y_s.at[zz], y_r.at[zz], base + py)
 
-    def dk_copy(zz, col):
-        return remote(
-            kv.at[0, :, zz, col], kv.at[0, :, zz, col], dk_s.at[zz], dk_r.at[zz], base + py
-        )
-
-    def dv_copy(zz, col):
-        return remote(
-            kv.at[1, :, zz, col], kv.at[1, :, zz, col], dv_s.at[zz], dv_r.at[zz], base + px
-        )
+    def dk_copy(col):
+        return remote(kv.at[0, :, z, col], kv.at[0, :, z, col], dk_s, dk_r, base + py)
+
+    def dv_copy(col):
+        return remote(kv.at[1, :, z, col], kv.at[1, :, z, col], dv_s, dv_r, base + px)
 
     def send_column(zz):
         @pl.when(has_up)
@@ -175,6 +174,18 @@
         local_states(peer)
         c.start()
     local_states(p)
+
+    def next_column(r):
+        @pl.when(r <= z)
+        def _():
+            up_copy(z - r).wait_recv()
+            send_column(z - r)
+
+    x_copy(z, px).wait_recv()
+    dk_copy(px).start()
+    y_copy(z, py).wait_recv()
+    dv_copy(py).start()
+    next_column(1)
 
     def load_queries(i, _):
         t0 = pl.multiple_of(i * step, step)
@@ -308,38 +319,38 @@
     def turn(r, _):
         zz = z - r
 
-        @pl.when(r < z)
-        def _():
-            up_copy(zz - 1).wait_recv()
-            send_column(zz - 1)
-
-        @pl.when(r <= z)
+        next_column(r + 2)
+
+        @pl.when(r == 0)
+        def _():
+            dk_copy(pd).wait_recv()
+            dv_copy(pd).wait_recv()
+
+        @pl.when(r > 0)
         def _():
             x_copy(zz, px).wait_recv()
-            dk_copy(zz, px).start()
             y_copy(zz, py).wait_recv()
-            dv_copy(zz, py).start()
-
-        @pl.when(r == z + 1)
+            up_diagonal(zz).wait_recv()
+
+        @pl.when(has_up)
+        def _():
+            up_diagonal(zz).start()
+
+        @pl.when(r == jnp.maximum(z - 1, 0))
         def _():
             state_chain()
 
+        @pl.when(r == 0)
+        def _():
+            attend(zz, True)
+
         @pl.when(r > 0)
         def _():
-            dk_copy(zz + 1, pd).wait_recv()
-            dv_copy(zz + 1, pd).wait_recv()
-
-        @pl.when(r == 1)
-        def _():
-            attend(zz + 1, True)
-
-        @pl.when(r > 1)
-        def _():
-            attend(zz + 1, False)
+            attend(zz, False)
 
         return 0
 
-    lax.fori_loop(0, z + 2, turn, 0)
+    lax.fori_loop(0, z + 1, turn, 0)
 
     for g in range(kv_local):
         for t in range(tiles):
@@ -357,24 +368,25 @@
 
     lax.fori_loop(0, rows // step, store_attn, 0)
 
-    for j in range(PARTS):
-        for i in range(GROUP - 1):
-            prior_copy(j, i).wait_recv()
     rowsq[...] = jnp.zeros(rowsq.shape, F32)
 
-    def outer(i, _):
-        ids = [i * together + u for u in range(together)]
+    def outer(owner, j):
+        hs = [j * part + u for u in range(part)]
+        ids = [owner * quarter + hh for hh in hs]
         qh = [head_rows(qf, h).astype(BF16) for h in ids]
         old = [head_rows(mixed, h) for h in ids]
-        ps = [prior[h // quarter, h % quarter] for h in ids]
+        ps = [prior[owner, hh] for hh in hs]
         os = [jnp.dot(q, x, preferred_element_type=F32) for q, x in zip(qh, ps)]
         new = [a + o * jnp.exp(colb[h]) for a, o, h in zip(old, os, ids)]
         for h, x in zip(ids, new):
             mixed[pl.ds(h, rows, stride=heads), :] = x
         rowsq[...] += sum(x * x for x in new)
-        return 0
-
-    lax.fori_loop(0, heads // together, outer, 0)
+
+    for j in range(PARTS):
+        outer(p, j)
+        for i in range(GROUP - 1):
+            prior_copy(j, i).wait_recv()
+            outer(peers[i], j)
     h_copies = [
         pltpu.make_async_remote_copy(
             src_ref=rowsq, dst_ref=rowsq_in.at[j - 1], send_sem=h_s.at[j - 1],
@@ -421,14 +433,15 @@
         @pl.when(has_up)
         def _():
             up_copy(zz).wait_send()
+            up_diagonal(zz).wait_send()
 
         x_copy(zz, p).wait_send()
         y_copy(zz, p).wait_send()
-        dk_copy(zz, px).wait_send()
-        dv_copy(zz, py).wait_send()
         return 0
 
     lax.fori_loop(0, z + 1, drain, 0)
+    dk_copy(px).wait_send()
+    dv_copy(py).wait_send()
 
 
 def local(planes, heads_dev, lin_query, lin_key, lin_value, log_decay, norm_gain,
@@ -469,7 +482,8 @@
             pltpu.VMEM((rows, HD), F32),
             pltpu.VMEM((max(heads_dev - 1, 1), rows, HD), F32),
         ]
-        + [dma((planes,))] * 10
+        + [dma((planes,))] * 8
+        + [dma] * 4
         + [dma((GROUP - 1,))] * 4
         + [dma(((GROUP - 1) * PARTS,))] * 2
         + [dma((PARTS,))] * 2

time: 80.5 us -> 72.8 us (0.904)
  Pallas kernels: 74.6 us -> 67 us
    pallas_call x1, Pallas kernels: 74.6 us -> 67 us  [local(): pl.pallas_call(functools.partial(kernel, planes, heads_dev), out_shape=(o...]
where the time goes in v3:
time: 72.8 us; the launch traced here: 72.7 us
  Pallas kernels  67 us (92%)
  local copies, waits for them, and re-layouts  5.03 us (7%)
    pallas_call x1, Pallas kernels, local(): pl.pallas_call(functools.partial(kernel, planes, heads_dev), out_shape=(o...  67 us
    unnamed x4, local copies, waits for them, and re-layouts  3.32 us
    transpose x1, local copies, waits for them, and re-layouts, local(): attn_value.transpose(1, 0, 2)  1.7 us

profile of v3, /device:TPU:29, one launch (start us, length us, event | category | flops | bytes accessed | tf_op | source)
XLA Modules:
  0.0 72.7 jit_solution(16868152026443622551)
XLA Ops:
  0.6 1.7 %copy_bitcast_fusion = (bf16[4,128,128]{2,1,0:T(8,128)(2,1)}, bf16[4,128,128]{2,1,0:T(8,128)(2,1)}) fusion(bf16[128,4,128]{2,1,0:T(4,128)(2,1)} %param.15, bf16[128,4,128]{2,1,0:T(4,128)(2,1)} %param.14), kind=kLoop, calls=%fused_computation | loop fusion | bytes 524288 | tf_op jit(solution)/shard_map/transpose | solution.py:496
  2.3 67.0 %mixers.1 = (bf16[128,32,128]{2,1,0:T(8,128)(2,1)}, bf16[128,32,128]{2,1,0:T(8,128)(2,1)}) custom-call(bf16[128,32,128]{2,1,0:T(8,128)(2,1)} %lq.1, bf16[128,32,128]{2,1,0:T(8,128)(2,1)} %lk.1, bf16[128,32,128]{2,1,0:T(8,128)(2,1)} %lv.1, f32[32,128]{1,0:T(8,128)} %decay.1, f32[32,128]{1,0:T(8,128)} %gain.1, bf16[128,32,128]{2,1,0:T(8,128)(2,1)} %aq.1, ...), custom_call_target="tpu_custom_call" | custom-call | tf_op jit(solution)/shard_map/mixers/pallas_call | solution.py:457
  69.3 0.0 copy-start
  69.3 2.4 %copy.16 = bf16[128,32,128]{2,1,0:T(8,128)(2,1)} copy(bf16[128,32,128]{2,1,0:T(8,128)(2,1)} %get-tuple-element.6) | data formatting | bytes 2097152
  71.7 0.0 copy-done
  71.7 1.0 %copy.17 = bf16[128,32,128]{2,1,0:T(8,128)(2,1)} copy(bf16[128,32,128]{2,1,0:T(8,128)(2,1)S(1)} %copy-done) | data formatting | bytes 2097152
Async XLA Ops:
  69.3 2.4 %copy-start = (bf16[128,32,128]{2,1,0:T(8,128)(2,1)S(1)}, bf16[128,32,128]{2,1,0:T(8,128)(2,1)}, u32[]{:S(2)}) copy-start(bf16[128,32,128]{2,1,0:T(8,128)(2,1)} %get-tuple-element.7) | copy-start | bytes 3145732

commit v4 on v3

--- a/solution.py
+++ b/solution.py
@@ -26,12 +26,19 @@
 
 
 def kernel(
-    planes, heads_dev, lq, lk, lv, decay, gain, aq, k_in, v_in, lin_out, attn_out,
+    planes, heads_dev, lq_in, lk_in, lv_in, decay, gain, aq_in, k_in, v_in, lin_hbm, attn_hbm,
+    lq, lk, lv, aq, lin_out, attn_out, in_sem, out_sem,
     qf, kf, vf, mixed, kv, qs, acc, m_ref, l_ref, ot, cum_ref, colb, lastb,
     sbuf, rs, prior, pr_send, carry, carry_out, rowsq, rowsq_in,
     z_s, z_r, zd_s, zd_r, x_s, x_r, y_s, y_r, dk_s, dk_r, dv_s, dv_r,
     s1_s, s1_r, la_s, la_r, s3_s, s3_r, c_s, c_r, h_s, h_r,
 ):
+    loads = [
+        pltpu.make_async_copy(src, dst, in_sem.at[i])
+        for i, (src, dst) in enumerate(((lk_in, lk), (lv_in, lv), (aq_in, aq), (lq_in, lq)))
+    ]
+    for c in loads:
+        c.start()
     rows, heads, _ = lq.shape
     kv_local = k_in.shape[0]
     group = heads // kv_local
@@ -97,15 +104,17 @@
     def dv_copy(col):
         return remote(kv.at[1, :, z, col], kv.at[1, :, z, col], dv_s, dv_r, base + px)
 
-    def send_column(zz):
-        @pl.when(has_up)
-        def _():
-            up_copy(zz).start()
-
+    def send_in_plane(zz):
         x_copy(zz, p).start()
         y_copy(zz, p).start()
 
-    send_column(z)
+    def send_up(zz):
+        @pl.when(has_up)
+        def _():
+            up_copy(zz).start()
+
+    send_in_plane(z)
+    send_up(z)
 
     step = 16
 
@@ -138,7 +147,9 @@
     for c in last_copies:
         c.start()
 
+    loads[0].wait()
     activate(lk, kf)
+    loads[1].wait()
     activate(lv, vf)
 
     together = min(4, quarter)
@@ -179,7 +190,7 @@
         @pl.when(r <= z)
         def _():
             up_copy(z - r).wait_recv()
-            send_column(z - r)
+            send_up(z - r)
 
     x_copy(z, px).wait_recv()
     dk_copy(px).start()
@@ -196,7 +207,9 @@
             qs[g, pl.ds(r0, step * group), :] = part.astype(BF16)
         return 0
 
+    loads[2].wait()
     lax.fori_loop(0, rows // step, load_queries, 0)
+    loads[3].wait()
     activate(lq, qf)
 
     def inner(i, _):
@@ -238,7 +251,7 @@
             ]
             if masked:
                 key_pos = lax.broadcasted_iota(jnp.int32, (span, MQ), 0)
-                col_pos = lax.broadcasted_iota(jnp.int32, (span, MQ), 1)
+                col_pos = lax.broadcasted_iota(jnp.int32, (1, MQ), 1)
                 ss = [
                     jnp.where(key_pos <= p * rows + (q0 + col_pos) // group, x, -1e30)
                     for q0, x in zip(starts, ss)
@@ -268,9 +281,12 @@
 
     part = quarter // PARTS
 
-    def carry_copy(j):
-        own = pl.ds(j * part, part)
-        return remote(carry_out.at[own], carry.at[own], c_s.at[j], c_r.at[j], me + GROUP)
+    sub = 2 if part % 2 == 0 else 1
+    piece = part // sub
+
+    def carry_copy(n):
+        own = pl.ds(n * piece, piece)
+        return remote(carry_out.at[own], carry.at[own], c_s.at[n], c_r.at[n], me + GROUP)
 
     def prior_copy(j, i):
         own = pl.ds(j * part, part)
@@ -289,14 +305,13 @@
         def _():
             carry[...] = jnp.zeros(carry.shape, BF16)
 
-        for j in range(PARTS):
+        for n in range(PARTS * sub):
 
             @pl.when(has_down)
             def _():
-                carry_copy(j).wait_recv()
-
-            def one(n, _):
-                hh = j * part + n
+                carry_copy(n).wait_recv()
+
+            for hh in range(n * piece, (n + 1) * piece):
                 h = p * quarter + hh
                 state = carry[hh].astype(F32)
                 for i in range(GROUP):
@@ -304,20 +319,22 @@
                     d = jnp.exp(lastb[i, pl.ds(h, 1), :])
                     state = d * state + rs[i, hh].astype(F32)
                 carry_out[hh] = state.astype(BF16)
-                return 0
-
-            lax.fori_loop(0, part, one, 0)
 
             @pl.when(has_up)
             def _():
-                carry_copy(j).start()
-
-            for i in range(GROUP - 1):
-                prior_copy(j, i).start()
+                carry_copy(n).start()
+
+            if n % sub == sub - 1:
+                for i in range(GROUP - 1):
+                    prior_copy(n // sub, i).start()
         prior[p] = pr_send[p]
 
     def turn(r, _):
         zz = z - r
+
+        @pl.when(r < z)
+        def _():
+            send_in_plane(zz - 1)
 
         next_column(r + 2)
 
@@ -336,7 +353,7 @@
         def _():
             up_diagonal(zz).start()
 
-        @pl.when(r == jnp.maximum(z - 1, 0))
+        @pl.when(r == z)
         def _():
             state_chain()
 
@@ -356,17 +373,6 @@
         for t in range(tiles):
             cols = slice(t * MQ, (t + 1) * MQ)
             ot[g, cols, :] = (acc[g, :, cols] / l_ref[g, :, cols]).T
-
-    def store_attn(i, _):
-        t0 = pl.multiple_of(i * step, step)
-        r0 = pl.multiple_of(t0 * group, step * group)
-        parts = [
-            ot[g, pl.ds(r0, step * group), :].reshape(step, group, HD) for g in range(kv_local)
-        ]
-        attn_out[pl.ds(t0, step)] = jnp.concatenate(parts, axis=1).astype(BF16)
-        return 0
-
-    lax.fori_loop(0, rows // step, store_attn, 0)
 
     rowsq[...] = jnp.zeros(rowsq.shape, F32)
 
@@ -398,6 +404,19 @@
     for c in h_copies:
         c.start()
 
+    def store_attn(i, _):
+        t0 = pl.multiple_of(i * step, step)
+        r0 = pl.multiple_of(t0 * group, step * group)
+        parts = [
+            ot[g, pl.ds(r0, step * group), :].reshape(step, group, HD) for g in range(kv_local)
+        ]
+        attn_out[pl.ds(t0, step)] = jnp.concatenate(parts, axis=1).astype(BF16)
+        return 0
+
+    lax.fori_loop(0, rows // step, store_attn, 0)
+    attn_store = pltpu.make_async_copy(attn_out, attn_hbm, out_sem.at[0])
+    attn_store.start()
+
     for c in h_copies:
         c.wait_recv()
     total = rowsq[...]
@@ -416,7 +435,16 @@
         lin_out[pl.ds(t0, step)] = (x * inv * gain[...][None]).astype(BF16)
         return 0
 
-    lax.fori_loop(0, rows // step, store_lin, 0)
+    halves = 2
+    lin_stores = []
+    for j in range(halves):
+        n = rows // step // halves
+        lax.fori_loop(j * n, (j + 1) * n, store_lin, 0)
+        own = pl.ds(j * n * step, n * step)
+        lin_stores.append(
+            pltpu.make_async_copy(lin_out.at[own], lin_hbm.at[own], out_sem.at[1 + j])
+        )
+        lin_stores[j].start()
 
     for c in last_copies + s1:
         c.wait_send()
@@ -426,8 +454,8 @@
 
     @pl.when(has_up)
     def _():
-        for j in range(PARTS):
-            carry_copy(j).wait_send()
+        for n in range(PARTS * sub):
+            carry_copy(n).wait_send()
 
     def drain(zz, _):
         @pl.when(has_up)
@@ -442,6 +470,9 @@
     lax.fori_loop(0, z + 1, drain, 0)
     dk_copy(px).wait_send()
     dv_copy(py).wait_send()
+    attn_store.wait()
+    for c in lin_stores:
+        c.wait()
 
 
 def local(planes, heads_dev, lin_query, lin_key, lin_value, log_decay, norm_gain,
@@ -451,15 +482,18 @@
     group = heads // kv_local
     quarter = heads // GROUP
     vmem = pl.BlockSpec(memory_space=pltpu.VMEM)
+    hbm = pl.BlockSpec(memory_space=pl.ANY)
     dma = pltpu.SemaphoreType.DMA
     out = jax.ShapeDtypeStruct(lin_query.shape, BF16)
     state = (GROUP, quarter, HD, HD)
     return pl.pallas_call(
         functools.partial(kernel, planes, heads_dev),
         out_shape=(out, out),
-        in_specs=[vmem] * 8,
-        out_specs=(vmem, vmem),
-        scratch_shapes=[
+        in_specs=[hbm, hbm, hbm, vmem, vmem, hbm, vmem, vmem],
+        out_specs=(hbm, hbm),
+        scratch_shapes=[pltpu.VMEM(lin_query.shape, BF16)] * 6
+        + [dma((4,)), dma((3,))]
+        + [
             pltpu.VMEM((rows * heads, HD), F32),
             pltpu.VMEM((rows * heads, HD), F32),
             pltpu.VMEM((rows * heads, HD), F32),
@@ -486,7 +520,7 @@
         + [dma] * 4
         + [dma((GROUP - 1,))] * 4
         + [dma(((GROUP - 1) * PARTS,))] * 2
-        + [dma((PARTS,))] * 2
+        + [dma((quarter,))] * 2
         + [dma((max(heads_dev - 1, 1),))] * 2,
         compiler_params=pltpu.CompilerParams(
             collective_id=0, has_side_effects=True, vmem_limit_bytes=56 * 2**20

time: 72.8 us -> 66.7 us (0.916)
  Pallas kernels: 67 us -> 60.9 us
    pallas_call x1, Pallas kernels: 67 us -> 60.9 us  [local(): pl.pallas_call(functools.partial(kernel, planes, heads_dev), out_shape=(o...]
where the time goes in v4:
time: 66.7 us; the launch traced here: 66.5 us
  Pallas kernels  60.9 us (91%)
  local copies, waits for them, and re-layouts  5.03 us (8%)
    pallas_call x1, Pallas kernels, local(): pl.pallas_call(functools.partial(kernel, planes, heads_dev), out_shape=(o...  60.9 us
    unnamed x4, local copies, waits for them, and re-layouts  3.32 us
    transpose x1, local copies, waits for them, and re-layouts, local(): attn_value.transpose(1, 0, 2)  1.7 us

profile of v4, /device:TPU:29, one launch (start us, length us, event | category | flops | bytes accessed | tf_op | source)
XLA Modules:
  0.0 66.5 jit_solution(18220617994057886797)
XLA Ops:
  0.6 1.7 %copy_bitcast_fusion = (bf16[4,128,128]{2,1,0:T(8,128)(2,1)}, bf16[4,128,128]{2,1,0:T(8,128)(2,1)}) fusion(bf16[128,4,128]{2,1,0:T(4,128)(2,1)} %param.15, bf16[128,4,128]{2,1,0:T(4,128)(2,1)} %param.14), kind=kLoop, calls=%fused_computation | loop fusion | bytes 524288 | tf_op jit(solution)/shard_map/transpose | solution.py:530
  2.3 60.9 %mixers.1 = (bf16[128,32,128]{2,1,0:T(8,128)(2,1)}, bf16[128,32,128]{2,1,0:T(8,128)(2,1)}) custom-call(bf16[128,32,128]{2,1,0:T(8,128)(2,1)} %lq_in.1, bf16[128,32,128]{2,1,0:T(8,128)(2,1)} %lk_in.1, bf16[128,32,128]{2,1,0:T(8,128)(2,1)} %lv_in.1, f32[32,128]{1,0:T(8,128)} %decay.1, f32[32,128]{1,0:T(8,128)} %gain.1, bf16[128,32,128]{2,1,0:T(8,128)(2,1)} %aq_in.1, ...), custom_call_target="tpu_custom_call" | custom-call | tf_op jit(solution)/shard_map/mixers/pallas_call | solution.py:489
  63.2 0.0 copy-start
  63.2 2.4 %copy.16 = bf16[128,32,128]{2,1,0:T(8,128)(2,1)} copy(bf16[128,32,128]{2,1,0:T(8,128)(2,1)} %get-tuple-element.6) | data formatting | bytes 2097152
  65.6 0.0 copy-done
  65.6 1.0 %copy.17 = bf16[128,32,128]{2,1,0:T(8,128)(2,1)} copy(bf16[128,32,128]{2,1,0:T(8,128)(2,1)S(1)} %copy-done) | data formatting | bytes 2097152
Async XLA Ops:
  63.2 2.4 %copy-start = (bf16[128,32,128]{2,1,0:T(8,128)(2,1)S(1)}, bf16[128,32,128]{2,1,0:T(8,128)(2,1)}, u32[]{:S(2)}) copy-start(bf16[128,32,128]{2,1,0:T(8,128)(2,1)} %get-tuple-element.7) | copy-start | bytes 3145732

commit v5 on v4

--- a/solution.py
+++ b/solution.py
@@ -27,7 +27,7 @@
 
 def kernel(
     planes, heads_dev, lq_in, lk_in, lv_in, decay, gain, aq_in, k_in, v_in, lin_hbm, attn_hbm,
-    lq, lk, lv, aq, lin_out, attn_out, in_sem, out_sem,
+    lq, lk, lv, aq, lin_out, attn_out, in_sem, out_sem, by_row,
     qf, kf, vf, mixed, kv, qs, acc, m_ref, l_ref, ot, cum_ref, colb, lastb,
     sbuf, rs, prior, pr_send, carry, carry_out, rowsq, rowsq_in,
     z_s, z_r, zd_s, zd_r, x_s, x_r, y_s, y_r, dk_s, dk_r, dv_s, dv_r,
@@ -40,7 +40,7 @@
     for c in loads:
         c.start()
     rows, heads, _ = lq.shape
-    kv_local = k_in.shape[0]
+    kv_local = k_in.shape[1]
     group = heads // kv_local
     quarter = heads // GROUP
     me = lax.axis_index("ctx")
@@ -61,8 +61,14 @@
             device_id={"ctx": ctx}, device_id_type=MESH,
         )
 
-    kv[0, :, z, p] = k_in[...]
-    kv[1, :, z, p] = v_in[...]
+    slots = -(-2 * kv_local // 8) * 8
+    both = [k_in[...].astype(F32), v_in[...].astype(F32)]
+    if slots > 2 * kv_local:
+        both.append(jnp.zeros((rows, slots - 2 * kv_local, HD), F32))
+    by_row[...] = jnp.concatenate(both, axis=1).reshape(rows * slots, HD)
+    for j in range(2):
+        for g in range(kv_local):
+            kv[j, g, z, p] = by_row[pl.ds(j * kv_local + g, rows, stride=slots), :].astype(BF16)
 
     barrier = pltpu.get_barrier_semaphore()
     for peer in peers:
@@ -235,49 +241,45 @@
     span = GROUP * rows
     tiles = rows * group // MQ
 
-    pair = 2
-    sets = tiles // pair
-
     def attend(zz, masked):
-        def body(i, _):
-            g = i // sets
-            starts = [pl.multiple_of(((i % sets) * pair + u) * MQ, MQ) for u in range(pair)]
-            cols = [pl.ds(q0, MQ) for q0 in starts]
+        def body(g, _):
+            cols = [pl.ds(t * MQ, MQ) for t in range(tiles)]
             k = kv[0, g, zz].reshape(span, HD)
             v = kv[1, g, zz].reshape(span, HD)
-            ss = [
-                lax.dot_general(k, qs[g, c, :], NT, preferred_element_type=F32) * scale
-                for c in cols
-            ]
-            if masked:
-                key_pos = lax.broadcasted_iota(jnp.int32, (span, MQ), 0)
-                col_pos = lax.broadcasted_iota(jnp.int32, (1, MQ), 1)
-                ss = [
-                    jnp.where(key_pos <= p * rows + (q0 + col_pos) // group, x, -1e30)
-                    for q0, x in zip(starts, ss)
-                ]
             m_old = [m_ref[g, :, c] for c in cols]
             l_old = [l_ref[g, :, c] for c in cols]
-            a_old = [acc[g, :, c] for c in cols]
-            m_new = [
-                jnp.maximum(m, jnp.max(x, axis=0, keepdims=True)) for m, x in zip(m_old, ss)
-            ]
-            alpha = [jnp.exp2(a - b) for a, b in zip(m_old, m_new)]
-            es = [jnp.exp2(x - m) for x, m in zip(ss, m_new)]
-            l_new = [
-                old * a + jnp.sum(e, axis=0, keepdims=True)
-                for old, a, e in zip(l_old, alpha, es)
-            ]
-            os = [
-                lax.dot_general(v, e.astype(BF16), TN, preferred_element_type=F32) for e in es
-            ]
-            for u, c in enumerate(cols):
-                m_ref[g, :, c] = m_new[u]
-                l_ref[g, :, c] = l_new[u]
-                acc[g, :, c] = a_old[u] * alpha[u] + os[u]
+
+            def scores(t):
+                s = lax.dot_general(k, qs[g, cols[t], :], NT, preferred_element_type=F32) * scale
+                if masked:
+                    key_pos = lax.broadcasted_iota(jnp.int32, (span, MQ), 0)
+                    col_pos = lax.broadcasted_iota(jnp.int32, (1, MQ), 1)
+                    s = jnp.where(key_pos <= p * rows + (t * MQ + col_pos) // group, s, -1e30)
+                return s
+
+            def probs(t, s):
+                m_new = jnp.maximum(m_old[t], jnp.max(s, axis=0, keepdims=True))
+                alpha = jnp.exp2(m_old[t] - m_new)
+                e = jnp.exp2(s - m_new)
+                m_ref[g, :, cols[t]] = m_new
+                l_ref[g, :, cols[t]] = l_old[t] * alpha + jnp.sum(e, axis=0, keepdims=True)
+                return e.astype(BF16), alpha
+
+            def values(t, e, alpha):
+                o = lax.dot_general(v, e, TN, preferred_element_type=F32)
+                acc[g, :, cols[t]] = acc[g, :, cols[t]] * alpha + o
+
+            ss, es = {}, {}
+            for t in range(tiles + 2):
+                if t < tiles:
+                    ss[t] = scores(t)
+                if 0 <= t - 2 < tiles:
+                    values(t - 2, *es.pop(t - 2))
+                if 0 <= t - 1 < tiles:
+                    es[t - 1] = probs(t - 1, ss.pop(t - 1))
             return 0
 
-        lax.fori_loop(0, kv_local * sets, body, 0)
+        lax.fori_loop(0, kv_local, body, 0)
 
     part = quarter // PARTS
 
@@ -475,6 +477,22 @@
         c.wait()
 
 
+def hand_over(lin_in, attn_in, lin_out, attn_out, sem):
+    pieces = 4
+    n = lin_in.shape[0] // pieces
+    copies = []
+    for i, (src, dst) in enumerate(((lin_in, lin_out), (attn_in, attn_out))):
+        for j in range(pieces):
+            own = pl.ds(j * n, n)
+            copies.append(
+                pltpu.make_async_copy(src.at[own], dst.at[own], sem.at[i * pieces + j])
+            )
+    for c in copies:
+        c.start()
+    for c in copies:
+        c.wait()
+
+
 def local(planes, heads_dev, lin_query, lin_key, lin_value, log_decay, norm_gain,
           attn_query, attn_key, attn_value):
     rows, heads, _ = lin_query.shape
@@ -486,13 +504,14 @@
     dma = pltpu.SemaphoreType.DMA
     out = jax.ShapeDtypeStruct(lin_query.shape, BF16)
     state = (GROUP, quarter, HD, HD)
-    return pl.pallas_call(
+    results = pl.pallas_call(
         functools.partial(kernel, planes, heads_dev),
         out_shape=(out, out),
         in_specs=[hbm, hbm, hbm, vmem, vmem, hbm, vmem, vmem],
         out_specs=(hbm, hbm),
         scratch_shapes=[pltpu.VMEM(lin_query.shape, BF16)] * 6
         + [dma((4,)), dma((3,))]
+        + [pltpu.VMEM((rows * (-(-2 * kv_local // 8) * 8), HD), F32)]
         + [
             pltpu.VMEM((rows * heads, HD), F32),
             pltpu.VMEM((rows * heads, HD), F32),
@@ -527,7 +546,16 @@
         ),
         name="mixers",
     )(lin_query, lin_key, lin_value, log_decay, norm_gain, attn_query,
-      attn_key.transpose(1, 0, 2), attn_value.transpose(1, 0, 2))
+      attn_key, attn_value)
+    return pl.pallas_call(
+        hand_over,
+        out_shape=(out, out),
+        in_specs=[hbm, hbm],
+        out_specs=(hbm, hbm),
+        scratch_shapes=[dma((8,))],
+        compiler_params=pltpu.CompilerParams(vmem_limit_bytes=56 * 2**20),
+        name="hand_over",
+    )(*results)
 
 
 def solution(mesh):

time: 66.7 us -> 125 us (1.87)
  Pallas kernels: 60.9 us -> 125 us
  local copies, waits for them, and re-layouts: 5.03 us -> 0 us
    pallas_call x0 -> x1, Pallas kernels: none -> 64.7 us  [local(): pl.pallas_call(hand_over, out_shape=(out, out), in_specs=[hbm, hbm], out_...]
    unnamed x4 -> x0, local copies, waits for them, and re-layouts: 3.32 us -> none
    transpose x1 -> x0, local copies, waits for them, and re-layouts: 1.7 us -> none  [local(): attn_value.transpose(1, 0, 2)]
where the time goes in v5:
time: 125 us
  Pallas kernels  125 us (100%)
    pallas_call x1, Pallas kernels, local(): pl.pallas_call(hand_over, out_shape=(out, out), in_specs=[hbm, hbm], out_...  64.7 us
    pallas_call x1, Pallas kernels, local(): pl.pallas_call(functools.partial(kernel, planes, heads_dev), out_shape=(o...  59.9 us

profile of v5, /device:TPU:29, one launch (start us, length us, event | category | flops | bytes accessed | tf_op | source)
XLA Modules:
  0.0 125.2 jit_solution(14090061669747986309)
XLA Ops:
  0.6 59.9 %mixers.1 = (bf16[128,32,128]{2,1,0:T(8,128)(2,1)}, bf16[128,32,128]{2,1,0:T(8,128)(2,1)}) custom-call(bf16[128,32,128]{2,1,0:T(8,128)(2,1)} %lq_in.1, bf16[128,32,128]{2,1,0:T(8,128)(2,1)} %lk_in.1, bf16[128,32,128]{2,1,0:T(8,128)(2,1)} %lv_in.1, f32[32,128]{1,0:T(8,128)} %decay.1, f32[32,128]{1,0:T(8,128)} %gain.1, bf16[128,32,128]{2,1,0:T(8,128)(2,1)} %aq_in.1, ...), custom_call_target="tpu_custom_call" | custom-call | tf_op jit(solution)/shard_map/mixers/pallas_call | solution.py:507
  60.5 64.7 %hand_over.1 = (bf16[128,32,128]{2,1,0:T(8,128)(2,1)}, bf16[128,32,128]{2,1,0:T(8,128)(2,1)}) custom-call(bf16[128,32,128]{2,1,0:T(8,128)(2,1)} %get-tuple-element.4.lin_in, bf16[128,32,128]{2,1,0:T(8,128)(2,1)} %get-tuple-element.5.attn_in), custom_call_target="tpu_custom_call" | custom-call | tf_op jit(solution)/shard_map/hand_over/pallas_call | solution.py:550

commit v6 on v5

--- a/solution.py
+++ b/solution.py
@@ -26,8 +26,8 @@
 
 
 def kernel(
-    planes, heads_dev, lq_in, lk_in, lv_in, decay, gain, aq_in, k_in, v_in, lin_hbm, attn_hbm,
-    lq, lk, lv, aq, lin_out, attn_out, in_sem, out_sem, by_row,
+    planes, heads_dev, lq_in, lk_in, lv_in, decay, aq_in, k_in, v_in, mixed_hbm, inverse, attn_hbm,
+    lq, lk, lv, aq, attn_out, in_sem, out_sem, by_row,
     qf, kf, vf, mixed, kv, qs, acc, m_ref, l_ref, ot, cum_ref, colb, lastb,
     sbuf, rs, prior, pr_send, carry, carry_out, rowsq, rowsq_in,
     z_s, z_r, zd_s, zd_r, x_s, x_r, y_s, y_r, dk_s, dk_r, dv_s, dv_r,
@@ -218,6 +218,13 @@
     loads[3].wait()
     activate(lq, qf)
 
+    dk_copy(pd).wait_recv()
+    dv_copy(pd).wait_recv()
+
+    @pl.when(has_up)
+    def _():
+        up_diagonal(z).start()
+
     def inner(i, _):
         ids = [i * together + u for u in range(together)]
         qh = [head_rows(qf, h).astype(BF16) for h in ids]
@@ -340,20 +347,16 @@
 
         next_column(r + 2)
 
-        @pl.when(r == 0)
-        def _():
-            dk_copy(pd).wait_recv()
-            dv_copy(pd).wait_recv()
-
         @pl.when(r > 0)
         def _():
+            up_diagonal(zz).wait_recv()
+
+            @pl.when(has_up)
+            def _():
+                up_diagonal(zz).start()
+
             x_copy(zz, px).wait_recv()
             y_copy(zz, py).wait_recv()
-            up_diagonal(zz).wait_recv()
-
-        @pl.when(has_up)
-        def _():
-            up_diagonal(zz).start()
 
         @pl.when(r == z)
         def _():
@@ -405,6 +408,8 @@
     ]
     for c in h_copies:
         c.start()
+    mixed_store = pltpu.make_async_copy(mixed, mixed_hbm, out_sem.at[1])
+    mixed_store.start()
 
     def store_attn(i, _):
         t0 = pl.multiple_of(i * step, step)
@@ -425,28 +430,7 @@
     for j in range(heads_dev - 1):
         total = total + rowsq_in[j]
     mean = jnp.sum(total, axis=1, keepdims=True) / (heads_dev * heads * HD)
-    for c in h_copies:
-        c.wait_send()
-    rowsq[...] = jnp.broadcast_to(lax.rsqrt(mean + 1e-06), (rows, HD))
-
-    def store_lin(i, _):
-        t0 = pl.multiple_of(i * step, step)
-        r0 = pl.multiple_of(t0 * heads, step * heads)
-        x = mixed[pl.ds(r0, step * heads), :].reshape(step, heads, HD)
-        inv = rowsq[pl.ds(t0, step), :].reshape(step, 1, HD)
-        lin_out[pl.ds(t0, step)] = (x * inv * gain[...][None]).astype(BF16)
-        return 0
-
-    halves = 2
-    lin_stores = []
-    for j in range(halves):
-        n = rows // step // halves
-        lax.fori_loop(j * n, (j + 1) * n, store_lin, 0)
-        own = pl.ds(j * n * step, n * step)
-        lin_stores.append(
-            pltpu.make_async_copy(lin_out.at[own], lin_hbm.at[own], out_sem.at[1 + j])
-        )
-        lin_stores[j].start()
+    inverse[...] = jnp.broadcast_to(lax.rsqrt(mean + 1e-06), (rows, HD))
 
     for c in last_copies + s1:
         c.wait_send()
@@ -472,25 +456,16 @@
     lax.fori_loop(0, z + 1, drain, 0)
     dk_copy(px).wait_send()
     dv_copy(py).wait_send()
+    for c in h_copies:
+        c.wait_send()
     attn_store.wait()
-    for c in lin_stores:
-        c.wait()
-
-
-def hand_over(lin_in, attn_in, lin_out, attn_out, sem):
-    pieces = 4
-    n = lin_in.shape[0] // pieces
-    copies = []
-    for i, (src, dst) in enumerate(((lin_in, lin_out), (attn_in, attn_out))):
-        for j in range(pieces):
-            own = pl.ds(j * n, n)
-            copies.append(
-                pltpu.make_async_copy(src.at[own], dst.at[own], sem.at[i * pieces + j])
-            )
-    for c in copies:
-        c.start()
-    for c in copies:
-        c.wait()
+    mixed_store.wait()
+
+
+def finish(mixed, inverse, gain, attn_in, lin_out, attn_out):
+    inv = inverse[...].reshape(inverse.shape[0], 1, HD)
+    lin_out[...] = (mixed[...] * inv * gain[...][None]).astype(BF16)
+    attn_out[...] = attn_in[...]
 
 
 def local(planes, heads_dev, lin_query, lin_key, lin_value, log_decay, norm_gain,
@@ -504,13 +479,17 @@
     dma = pltpu.SemaphoreType.DMA
     out = jax.ShapeDtypeStruct(lin_query.shape, BF16)
     state = (GROUP, quarter, HD, HD)
-    results = pl.pallas_call(
+    mixed, inverse, attn = pl.pallas_call(
         functools.partial(kernel, planes, heads_dev),
-        out_shape=(out, out),
-        in_specs=[hbm, hbm, hbm, vmem, vmem, hbm, vmem, vmem],
-        out_specs=(hbm, hbm),
-        scratch_shapes=[pltpu.VMEM(lin_query.shape, BF16)] * 6
-        + [dma((4,)), dma((3,))]
+        out_shape=(
+            jax.ShapeDtypeStruct((rows * heads, HD), F32),
+            jax.ShapeDtypeStruct((rows, HD), F32),
+            out,
+        ),
+        in_specs=[hbm, hbm, hbm, vmem, hbm, vmem, vmem],
+        out_specs=(hbm, vmem, hbm),
+        scratch_shapes=[pltpu.VMEM(lin_query.shape, BF16)] * 5
+        + [dma((4,)), dma((2,))]
         + [pltpu.VMEM((rows * (-(-2 * kv_local // 8) * 8), HD), F32)]
         + [
             pltpu.VMEM((rows * heads, HD), F32),
@@ -545,17 +524,24 @@
             collective_id=0, has_side_effects=True, vmem_limit_bytes=56 * 2**20
         ),
         name="mixers",
-    )(lin_query, lin_key, lin_value, log_decay, norm_gain, attn_query,
+    )(lin_query, lin_key, lin_value, log_decay, attn_query,
       attn_key, attn_value)
+    tile = rows // 4
+    block = pl.BlockSpec((tile, heads, HD), lambda i: (i, 0, 0))
     return pl.pallas_call(
-        hand_over,
+        finish,
+        grid=(rows // tile,),
         out_shape=(out, out),
-        in_specs=[hbm, hbm],
-        out_specs=(hbm, hbm),
-        scratch_shapes=[dma((8,))],
+        in_specs=[
+            block,
+            pl.BlockSpec((tile, HD), lambda i: (i, 0)),
+            pl.BlockSpec((heads, HD), lambda i: (0, 0)),
+            block,
+        ],
+        out_specs=(block, block),
         compiler_params=pltpu.CompilerParams(vmem_limit_bytes=56 * 2**20),
-        name="hand_over",
-    )(*results)
+        name="finish",
+    )(mixed.reshape(rows, heads, HD), inverse, norm_gain, attn)
 
 
 def solution(mesh):

time: 125 us -> 70.8 us (0.57)
  Pallas kernels: 125 us -> 69.3 us
    pallas_call x2, Pallas kernels: 125 us -> 69.3 us  [the longest x1 65.3 us: local(): pl.pallas_call(functools.partial(kernel, planes, heads_dev), out_shape=(j...]
where the time goes in v6:
time: 70.8 us; the launch traced here: 69.9 us
  Pallas kernels  69.3 us (98%)
    pallas_call x1, Pallas kernels, local(): pl.pallas_call(functools.partial(kernel, planes, heads_dev), out_shape=(j...  65.3 us
    pallas_call x1, Pallas kernels, local(): pl.pallas_call(finish, grid=(rows // tile,), out_shape=(out, out), in_spe...  4 us

profile of v6, /device:TPU:29, one launch (start us, length us, event | category | flops | bytes accessed | tf_op | source)
XLA Modules:
  0.0 69.9 jit_solution(2199909356476853140)
XLA Ops:
  0.6 65.3 %mixers.1 = (f32[4096,128]{1,0:T(8,128)}, f32[128,128]{1,0:T(8,128)}, bf16[128,32,128]{2,1,0:T(8,128)(2,1)}) custom-call(bf16[128,32,128]{2,1,0:T(8,128)(2,1)} %lq_in.1, bf16[128,32,128]{2,1,0:T(8,128)(2,1)} %lk_in.1, bf16[128,32,128]{2,1,0:T(8,128)(2,1)} %lv_in.1, f32[32,128]{1,0:T(8,128)} %decay.1, bf16[128,32,128]{2,1,0:T(8,128)(2,1)} %aq_in.1, ...), custom_call_target="tpu_custom_call" | custom-call | tf_op jit(solution)/shard_map/mixers/pallas_call | solution.py:482
  65.9 4.0 %finish.1 = (bf16[128,32,128]{2,1,0:T(8,128)(2,1)}, bf16[128,32,128]{2,1,0:T(8,128)(2,1)}) custom-call(f32[128,32,128]{2,1,0:T(8,128)} %bitcast.1, f32[128,128]{1,0:T(8,128)} %get-tuple-element.6.inverse, f32[32,128]{1,0:T(8,128)} %gain.1, bf16[128,32,128]{2,1,0:T(8,128)(2,1)} %get-tuple-element.7.attn_in), custom_call_target="tpu_custom_call" | custom-call | tf_op jit(solution)/shard_map/finish/pallas_call | solution.py:531

commit v7 on v5

--- a/solution.py
+++ b/solution.py
@@ -477,19 +477,22 @@
         c.wait()
 
 
-def hand_over(lin_in, attn_in, lin_out, attn_out, sem):
+def hand_over(lin_in, attn_in, lin_out, attn_out, lin_held, attn_held, load_sem, store_sem):
     pieces = 4
     n = lin_in.shape[0] // pieces
-    copies = []
-    for i, (src, dst) in enumerate(((lin_in, lin_out), (attn_in, attn_out))):
+    loads, stores = [], []
+    arrays = ((lin_in, lin_held, lin_out), (attn_in, attn_held, attn_out))
+    for i, (src, held, dst) in enumerate(arrays):
         for j in range(pieces):
-            own = pl.ds(j * n, n)
-            copies.append(
-                pltpu.make_async_copy(src.at[own], dst.at[own], sem.at[i * pieces + j])
-            )
-    for c in copies:
+            own, k = pl.ds(j * n, n), i * pieces + j
+            loads.append(pltpu.make_async_copy(src.at[own], held.at[own], load_sem.at[k]))
+            stores.append(pltpu.make_async_copy(held.at[own], dst.at[own], store_sem.at[k]))
+    for c in loads:
         c.start()
-    for c in copies:
+    for load, store in zip(loads, stores):
+        load.wait()
+        store.start()
+    for c in stores:
         c.wait()
 
 
@@ -552,7 +555,7 @@
         out_shape=(out, out),
         in_specs=[hbm, hbm],
         out_specs=(hbm, hbm),
-        scratch_shapes=[dma((8,))],
+        scratch_shapes=[pltpu.VMEM(out.shape, BF16)] * 2 + [dma((8,))] * 2,
         compiler_params=pltpu.CompilerParams(vmem_limit_bytes=56 * 2**20),
         name="hand_over",
     )(*results)

time: 125 us -> 63.1 us (0.50)
  Pallas kernels: 125 us -> 62.3 us
    pallas_call x1, Pallas kernels: 64.7 us -> 2.4 us  [local(): pl.pallas_call(hand_over, out_shape=(out, out), in_specs=[hbm, hbm], out_...]
where the time goes in v7:
time: 63.1 us; the launch traced here: 62.9 us
  Pallas kernels  62.3 us (99%)
  between operations  0.64 us (1%)
    pallas_call x1, Pallas kernels, local(): pl.pallas_call(functools.partial(kernel, planes, heads_dev), out_shape=(o...  59.9 us
    pallas_call x1, Pallas kernels, local(): pl.pallas_call(hand_over, out_shape=(out, out), in_specs=[hbm, hbm], out_...  2.4 us

profile of v7, /device:TPU:29, one launch (start us, length us, event | category | flops | bytes accessed | tf_op | source)
XLA Modules:
  0.0 62.9 jit_solution(2178516444306085495)
XLA Ops:
  0.6 59.9 %mixers.1 = (bf16[128,32,128]{2,1,0:T(8,128)(2,1)}, bf16[128,32,128]{2,1,0:T(8,128)(2,1)}) custom-call(bf16[128,32,128]{2,1,0:T(8,128)(2,1)} %lq_in.1, bf16[128,32,128]{2,1,0:T(8,128)(2,1)} %lk_in.1, bf16[128,32,128]{2,1,0:T(8,128)(2,1)} %lv_in.1, f32[32,128]{1,0:T(8,128)} %decay.1, f32[32,128]{1,0:T(8,128)} %gain.1, bf16[128,32,128]{2,1,0:T(8,128)(2,1)} %aq_in.1, ...), custom_call_target="tpu_custom_call" | custom-call | tf_op jit(solution)/shard_map/mixers/pallas_call | solution.py:510
  60.5 2.4 %hand_over.1 = (bf16[128,32,128]{2,1,0:T(8,128)(2,1)}, bf16[128,32,128]{2,1,0:T(8,128)(2,1)}) custom-call(bf16[128,32,128]{2,1,0:T(8,128)(2,1)} %get-tuple-element.4.lin_in, bf16[128,32,128]{2,1,0:T(8,128)(2,1)} %get-tuple-element.5.attn_in), custom_call_target="tpu_custom_call" | custom-call | tf_op jit(solution)/shard_map/hand_over/pallas_call | solution.py:553

commit v8 on v7

--- a/solution.py
+++ b/solution.py
@@ -187,9 +187,14 @@
         remote(sbuf.at[peer], rs.at[p], s1_s.at[i], s1_r.at[i], base + peer)
         for i, peer in enumerate(peers)
     ]
-    for peer, c in zip(peers, s1):
-        local_states(peer)
-        c.start()
+    for n, i in enumerate((2, 0, 1)):
+        local_states(peers[i])
+        s1[i].start()
+        if n == 1:
+            x_copy(z, px).wait_recv()
+            dk_copy(px).start()
+            y_copy(z, py).wait_recv()
+            dv_copy(py).start()
     local_states(p)
 
     def next_column(r):
@@ -198,10 +203,6 @@
             up_copy(z - r).wait_recv()
             send_up(z - r)
 
-    x_copy(z, px).wait_recv()
-    dk_copy(px).start()
-    y_copy(z, py).wait_recv()
-    dv_copy(py).start()
     next_column(1)
 
     def load_queries(i, _):

time: 63.1 us -> 65.8 us (1.043)
  Pallas kernels: 62.3 us -> 65 us
    pallas_call x1, Pallas kernels: 59.9 us -> 62.6 us  [local(): pl.pallas_call(functools.partial(kernel, planes, heads_dev), out_shape=(o...]
where the time goes in v8:
time: 65.8 us; the launch traced here: 65.6 us
  Pallas kernels  65 us (99%)
    pallas_call x1, Pallas kernels, local(): pl.pallas_call(functools.partial(kernel, planes, heads_dev), out_shape=(o...  62.6 us
    pallas_call x1, Pallas kernels, local(): pl.pallas_call(hand_over, out_shape=(out, out), in_specs=[hbm, hbm], out_...  2.4 us

profile of v8, /device:TPU:29, one launch (start us, length us, event | category | flops | bytes accessed | tf_op | source)
XLA Modules:
  0.0 65.6 jit_solution(5610026046161676760)
XLA Ops:
  0.6 62.6 %mixers.1 = (bf16[128,32,128]{2,1,0:T(8,128)(2,1)}, bf16[128,32,128]{2,1,0:T(8,128)(2,1)}) custom-call(bf16[128,32,128]{2,1,0:T(8,128)(2,1)} %lq_in.1, bf16[128,32,128]{2,1,0:T(8,128)(2,1)} %lk_in.1, bf16[128,32,128]{2,1,0:T(8,128)(2,1)} %lv_in.1, f32[32,128]{1,0:T(8,128)} %decay.1, f32[32,128]{1,0:T(8,128)} %gain.1, bf16[128,32,128]{2,1,0:T(8,128)(2,1)} %aq_in.1, ...), custom_call_target="tpu_custom_call" | custom-call | tf_op jit(solution)/shard_map/mixers/pallas_call | solution.py:511
  63.2 2.4 %hand_over.1 = (bf16[128,32,128]{2,1,0:T(8,128)(2,1)}, bf16[128,32,128]{2,1,0:T(8,128)(2,1)}) custom-call(bf16[128,32,128]{2,1,0:T(8,128)(2,1)} %get-tuple-element.4.lin_in, bf16[128,32,128]{2,1,0:T(8,128)(2,1)} %get-tuple-element.5.attn_in), custom_call_target="tpu_custom_call" | custom-call | tf_op jit(solution)/shard_map/hand_over/pallas_call | solution.py:554

commit v9 on v7

--- a/solution.py
+++ b/solution.py
@@ -340,6 +340,10 @@
 
         next_column(r + 2)
 
+        @pl.when(z == 0)
+        def _():
+            state_chain()
+
         @pl.when(r == 0)
         def _():
             dk_copy(pd).wait_recv()
@@ -355,7 +359,7 @@
         def _():
             up_diagonal(zz).start()
 
-        @pl.when(r == z)
+        @pl.when(jnp.logical_and(r == z, z > 0))
         def _():
             state_chain()
 

time: 63.1 us -> 64.5 us (1.022); the launches traced: 62.9 us -> 63.4 us
  no operation moved by 1% of the time
where the time goes in v9:
time: 64.5 us; the launch traced here: 63.4 us
  Pallas kernels  62.7 us (97%)
    pallas_call x1, Pallas kernels, local(): pl.pallas_call(functools.partial(kernel, planes, heads_dev), out_shape=(o...  60.4 us
    pallas_call x1, Pallas kernels, local(): pl.pallas_call(hand_over, out_shape=(out, out), in_specs=[hbm, hbm], out_...  2.4 us

profile of v9, /device:TPU:29, one launch (start us, length us, event | category | flops | bytes accessed | tf_op | source)
XLA Modules:
  0.0 63.4 jit_solution(7790276073570758085)
XLA Ops:
  0.6 60.4 %mixers.1 = (bf16[128,32,128]{2,1,0:T(8,128)(2,1)}, bf16[128,32,128]{2,1,0:T(8,128)(2,1)}) custom-call(bf16[128,32,128]{2,1,0:T(8,128)(2,1)} %lq_in.1, bf16[128,32,128]{2,1,0:T(8,128)(2,1)} %lk_in.1, bf16[128,32,128]{2,1,0:T(8,128)(2,1)} %lv_in.1, f32[32,128]{1,0:T(8,128)} %decay.1, f32[32,128]{1,0:T(8,128)} %gain.1, bf16[128,32,128]{2,1,0:T(8,128)(2,1)} %aq_in.1, ...), custom_call_target="tpu_custom_call" | custom-call | tf_op jit(solution)/shard_map/mixers/pallas_call | solution.py:514
  61.0 2.4 %hand_over.1 = (bf16[128,32,128]{2,1,0:T(8,128)(2,1)}, bf16[128,32,128]{2,1,0:T(8,128)(2,1)}) custom-call(bf16[128,32,128]{2,1,0:T(8,128)(2,1)} %get-tuple-element.4.lin_in, bf16[128,32,128]{2,1,0:T(8,128)(2,1)} %get-tuple-element.5.attn_in), custom_call_target="tpu_custom_call" | custom-call | tf_op jit(solution)/shard_map/hand_over/pallas_call | solution.py:557
